TPU v7x, 128 devices: a whole 4x4x4 slice. The times are simulated.
128 devices in a mesh: fsdp: 32 (over z, x, core), feat: 4 (over y).
Axes of the slice: x: 4, y: 4, z: 4, core: 2. Of those that a mesh axis runs over, the one named last changes fastest.
Arguments:
- table_cells: bfloat16 [1536, 256, 192], P(('fsdp', 'feat'))
- attn_weights: bfloat16 [8, 192, 192], P(None, 'fsdp')
- hidden_up_weight: bfloat16 [192, 384], P('fsdp'), may hold values from -0.4375 to 0.4375
- hidden_down_weight: bfloat16 [384, 192], P('fsdp'), may hold values from -0.3125 to 0.3125
- norm_gains: float32 [3, 192], replicated, may hold values from 0.25 to 1.75
- train_count: int32 [1], replicated, may hold values from 384 to 1152
- feature_count: int32 [1], replicated, may hold values from 128 to 256
Outputs:
- layer_out: bfloat16 [1536, 256, 192], P(('fsdp', 'feat'))
Inputs may be any that keep to these rules, and one draw needn't show every extreme that they name: Rows 0 to train_count - 1 are the training rows. Features 0 to feature_count - 1 are real, the others padding.
All inputs are finite; a program needn't handle non-finite values.
Results may differ from a plain program's by a relative error of at most 0.012.
The roundings to bfloat16 on the way count: a program that leaves them out, or rounds other values in their place, can miss the bound.
Values may be sent and summed in bfloat16 or wider, within the bound.
A program may use at most 128 MiB of HBM per device.

v0:
```python
import jax
import jax.numpy as jnp
from jax import lax
from jax.sharding import PartitionSpec as P

HEADS = 6


EPS = 1e-05
NEGATIVE = -1e30


def normalize(value_rows, gain):
    floats = value_rows.astype(jnp.float32)
    average = jnp.mean(floats, axis=-1, keepdims=True)
    centered = floats - average
    variance = jnp.mean(centered * centered, axis=-1, keepdims=True)
    return (centered * lax.rsqrt(variance + EPS) * gain).astype(jnp.bfloat16)


def softmax_rows(scores, live):
    masked = jnp.where(live, scores, NEGATIVE)
    row_maximum = jnp.max(masked, axis=-1, keepdims=True)
    exponent = jnp.exp(masked - row_maximum)
    return (exponent / jnp.sum(exponent, axis=-1, keepdims=True)).astype(jnp.bfloat16)


def project(normed, weight):
    model_width = normed.shape[-1]
    product = jnp.dot(normed.reshape(-1, model_width), weight, preferred_element_type=jnp.float32)
    return product.astype(jnp.bfloat16).reshape(normed.shape[:-1] + (weight.shape[1],))


def output_proj(attended_rows, residual, weight):
    model_width = attended_rows.shape[-1]
    product = jnp.dot(
        attended_rows.reshape(-1, model_width), weight, preferred_element_type=jnp.float32
    )
    return (residual.astype(jnp.float32) + product.reshape(residual.shape)).astype(jnp.bfloat16)


def feature_attention(table_cells, normed, weights, feat_live):
    model_width = normed.shape[-1]
    head_size = model_width // HEADS
    queries = project(normed, weights[0])
    keys = project(normed, weights[1])
    value_rows = project(normed, weights[2])
    outputs = []
    for index_head in range(HEADS):
        training_extent = slice(index_head * head_size, (index_head + 1) * head_size)
        scores = jnp.einsum(
            "rqe,rke->rqk",
            queries[..., training_extent],
            keys[..., training_extent],
            preferred_element_type=jnp.float32,
        ) * head_size ** (-0.5)
        attention_probabilities = softmax_rows(scores, feat_live[None, None, :])
        outputs.append(
            jnp.einsum(
                "rqk,rke->rqe",
                attention_probabilities,
                value_rows[..., training_extent],
                preferred_element_type=jnp.float32,
            ).astype(jnp.bfloat16)
        )
    return output_proj(jnp.concatenate(outputs, axis=-1), table_cells, weights[3])


def sample_attention(column_block, normed, weights, row_live):
    all_rows, feat_here, model_width = normed.shape
    head_size = model_width // HEADS
    queries = project(normed, weights[4])
    keys = project(normed, weights[5])
    value_rows = project(normed, weights[6])
    block_count = max(1, all_rows // 512)
    block_rows = all_rows // block_count
    query_blocks = queries.reshape(block_count, block_rows, feat_here, model_width)

    def one_block(query_block):
        outputs = []
        for index_head in range(HEADS):
            training_extent = slice(index_head * head_size, (index_head + 1) * head_size)
            scores = jnp.einsum(
                "vsg,psg->svp",
                query_block[..., training_extent],
                keys[..., training_extent],
                preferred_element_type=jnp.float32,
            ) * head_size ** (-0.5)
            attention_probabilities = softmax_rows(scores, row_live[None, None, :])
            outputs.append(
                jnp.einsum(
                    "tdj,jtn->dtn",
                    attention_probabilities,
                    value_rows[..., training_extent],
                    preferred_element_type=jnp.float32,
                ).astype(jnp.bfloat16)
            )
        return jnp.concatenate(outputs, axis=-1)

    attended_rows = lax.map(one_block, query_blocks).reshape(all_rows, feat_here, model_width)
    return output_proj(attended_rows, column_block, weights[7])


def feed_forward(value_rows, gain, w_in, w_out):
    model_width = value_rows.shape[-1]
    normed = normalize(value_rows, gain)
    hidden = jnp.dot(normed.reshape(-1, model_width), w_in, preferred_element_type=jnp.float32)
    activated = jax.nn.gelu(hidden).astype(jnp.bfloat16)
    result = value_rows.astype(jnp.float32) + jnp.dot(
        activated, w_out, preferred_element_type=jnp.float32
    ).reshape(value_rows.shape)
    return result.astype(jnp.bfloat16)


def local(
    table_cells,
    attn_weights,
    hidden_up_weight,
    hidden_down_weight,
    norm_gains,
    train_count,
    feature_count,
):
    weights, w_in, w_out = (
        lax.all_gather(attn_weights, "fsdp", axis=1, tiled=True),
        lax.all_gather(hidden_up_weight, "fsdp", axis=0, tiled=True),
        lax.all_gather(hidden_down_weight, "fsdp", axis=0, tiled=True),
    )
    feat_live = jnp.arange(table_cells.shape[1]) < feature_count[0]
    normed_one = normalize(table_cells, norm_gains[0])
    mixed_rows = feature_attention(table_cells, normed_one, weights, feat_live)
    fsdp_size = lax.axis_size("fsdp")
    groups = lax.axis_size("feat")
    row_dev, feat_total, model_width = table_cells.shape
    devices_all = fsdp_size * groups
    all_rows = row_dev * devices_all
    train_limit = train_count[0]
    row_index = jnp.arange(all_rows)
    split_cells = mixed_rows.reshape(row_dev, devices_all, feat_total // devices_all, model_width)
    column_block = lax.all_to_all(
        split_cells, ("fsdp", "feat"), split_axis=1, concat_axis=0, tiled=True
    )
    rows_here, single, feat_here, width_here = column_block.shape
    owner_column_block = column_block.reshape(rows_here, feat_here, width_here)
    normed_two = normalize(owner_column_block, norm_gains[1])
    sampled = sample_attention(owner_column_block, normed_two, weights, row_index < train_limit)
    at_owners = sampled.reshape(rows_here, single, feat_here, width_here)
    returned = lax.all_to_all(at_owners, ("fsdp", "feat"), split_axis=0, concat_axis=1, tiled=True)
    returned = returned.reshape(row_dev, feat_total, model_width)
    returned = feed_forward(returned, norm_gains[2], w_in, w_out)
    return returned


def solution(mesh):
    in_specs = (
        P(("fsdp", "feat"), None, None),
        P(None, "fsdp", None),
        P("fsdp", None),
        P("fsdp", None),
        P(),
        P(),
        P(),
    )
    out_specs = P(("fsdp", "feat"), None, None)
    return jax.shard_map(local, mesh=mesh, in_specs=in_specs, out_specs=out_specs, check_vma=False)
```

profile of v0, /device:TPU:1, one launch (start us, length us, event | category | flops | bytes accessed | tf_op | source)
XLA Modules:
  0.0 370.8 jit_solution(5374347418670035218)
XLA Ops:
  0.0 27.7 %all_gather.9 = bf16[8,192,192]{2,0,1:T(8,128)(2,1)S(1)} all-gather(bf16[8,6,192]{2,0,1:T(8,128)(2,1)} %param.10), channel_id=1, replica_groups=mesh['fsdp'=32,'feat'=4] {'fsdp'}, dimensions={1}, use_global_device_ids=true | all-gather | bytes 608256 | tf_op jit(solution)/shard_map/all_gather | solution.py:125
  47.1 3.9 %fusion.417 = (f32[12,256]{1,0:T(8,128)S(1)}, f32[12,256,256]{1,2,0:T(8,128)}) fusion(pred[256]{0:T(512)(128)(4,1)S(1)} %iota_compare_fusion.1, bf16[12,256,32]{1,0,2:T(8,128)(2,1)} %get-tuple-element.136, bf16[12,256,32]{1,0,2:T(8,128)(2,1)} %get-tuple-element.106), kind=kOutput, calls=%fused_computation.353 | convolution fusion | flops 53477632 | bytes 3551488 | tf_op jit(solution)/shard_map/sub | solution.py:24
  51.0 4.0 %fusion.426 = (f32[12,256]{1,0:T(8,128)S(1)}, f32[12,256,256]{1,2,0:T(8,128)}) fusion(pred[256]{0:T(512)(128)(4,1)S(1)} %iota_compare_fusion.1, bf16[12,256,32]{1,0,2:T(8,128)(2,1)} %get-tuple-element.137, bf16[12,256,32]{1,0,2:T(8,128)(2,1)} %get-tuple-element.105), kind=kOutput, calls=%fused_computation.354 | convolution fusion | flops 53477632 | bytes 3551488 | tf_op jit(solution)/shard_map/sub | solution.py:24
  55.0 4.0 %fusion.435 = (f32[12,256]{1,0:T(8,128)S(1)}, f32[12,256,256]{1,2,0:T(8,128)}) fusion(pred[256]{0:T(512)(128)(4,1)S(1)} %iota_compare_fusion.1, bf16[12,256,32]{1,0,2:T(8,128)(2,1)} %get-tuple-element.138, bf16[12,256,32]{1,0,2:T(8,128)(2,1)} %get-tuple-element.104), kind=kOutput, calls=%fused_computation.355 | convolution fusion | flops 53477632 | bytes 3551488 | tf_op jit(solution)/shard_map/sub | solution.py:24
  84.9 7.2 %all-to-all-start = ((bf16[12,128,2,192]{3,2,0,1:T(2,128)(2,1)}), bf16[12,128,2,192]{3,2,0,1:T(2,128)(2,1)S(1)}, u32[]{:S(2)}, u32[]{:S(2)}) async-start(bf16[12,128,2,192]{3,2,0,1:T(2,128)(2,1)} %copy.182), calls=%async_computation | async-start | bytes 3145728 | tf_op jit(solution)/shard_map/all_to_all | solution.py:140
  92.9 24.1 %all-to-all-done = bf16[12,128,2,192]{3,2,0,1:T(2,128)(2,1)S(1)} async-done(((bf16[12,128,2,192]{3,2,0,1:T(2,128)(2,1)}), bf16[12,128,2,192]{3,2,0,1:T(2,128)(2,1)S(1)}, u32[]{:S(2)}, u32[]{:S(2)}) %all-to-all-start) | async-done | bytes 1179680 | tf_op jit(solution)/shard_map/all_to_all | solution.py:140
  118.9 4.0 %multiply_reduce_fusion.1 = f32[128,12,2]{2,1,0:T(8,128)S(1)} fusion(bf16[12,128,2,192]{3,2,0,1:T(2,128)(2,1)S(1)} %all-to-all-done, f32[128,12,2]{2,1,0:T(8,128)S(1)} %broadcast_multiply_fusion.1), kind=kLoop, calls=%fused_computation.190 | loop fusion | flops 2356224 | bytes 1204224 | tf_op jit(solution)/shard_map/reduce_sum | solution.py:17
  123.1 3.9 %multiply_convert_fusion.1 = bf16[128,12,1,2,192]{4,3,1,0,2:T(2,128)(2,1)S(1)} fusion(bf16[12,128,2,192]{3,2,0,1:T(2,128)(2,1)S(1)} %all-to-all-done, f32[192]{0:T(256)S(1)} %bitcast.148, f32[128,12,2]{2,1,0:T(8,128)S(1)} %add_rsqrt_fusion.1, f32[128,12,2]{2,1,0:T(8,128)S(1)} %broadcast_multiply_fusion.1), kind=kLoop, calls=%fused_computation.189 | loop fusion | flops 2949120 | bytes 2384640 | tf_op jit(solution)/shard_map/convert_element_type | solution.py:18
  134.0 4.9 %copy.190 = bf16[1536,2,192]{0,2,1:T(8,128)(2,1)} copy(bf16[1536,2,192]{2,1,0:T(2,128)(2,1)} %reshape.234) | data formatting | bytes 2359296
  144.4 4.9 %copy.191 = bf16[1536,2,192]{0,2,1:T(8,128)(2,1)} copy(bf16[1536,2,192]{2,1,0:T(2,128)(2,1)} %reshape.235) | data formatting | bytes 2359296
  152.6 105.7 %while.11 = (s32[]{:T(128)}, bf16[3,512,2,192]{1,3,2,0:T(8,128)(2,1)}, bf16[3,512,2,192]{1,3,2,0:T(8,128)(2,1)S(1)}, bf16[1536,2,192]{0,2,1:T(8,128)(2,1)}, bf16...) while((s32[]{:T(128)}, bf16[3,512,2,192]{1,3,2,0:T(8,128)(2,1)}, ...), condition=%wide.region_29.30_spmd.clone, body=%wide.region_16.29_spmd.clone.sunk | while | flops 1897096704 | bytes 11085937 | solution.py:100
  162.1 3.3 fusion.556
  167.5 3.3 fusion.558
  172.9 3.3 fusion.560
  197.1 3.3 fusion.556
  232.2 3.3 fusion.556
  262.0 3.3 copy.194
  270.7 3.9 %all-to-all-start.1 = ((bf16[1536,1,2,192]{3,2,1,0:T(2,128)(2,1)}), bf16[1536,1,2,192]{3,2,1,0:T(2,128)(2,1)S(1)}, u32[]{:S(2)}, u32[]{:S(2)}) async-start(bf16[1536,1,2,192]{3,2,1,0:T(2,128)(2,1)} %copy.195), calls=%async_computation.1 | async-start | bytes 3145728 | tf_op jit(solution)/shard_map/all_to_all | solution.py:148
  274.6 39.1 %all-gather.1 = bf16[32,12,192]{2,1,0:T(8,128)(2,1)S(1)} all-gather(bf16[1,12,192]{2,1,0:T(8,128)(2,1)S(1)} %bitcast.145), channel_id=1, replica_groups=mesh['fsdp'=32,'feat'=4] {'fsdp'}, dimensions={0}, use_global_device_ids=true | all-gather | bytes 152064 | tf_op jit(solution)/shard_map/all_gather | solution.py:127
  313.8 22.8 %all-gather = bf16[32,6,384]{2,1,0:T(8,128)(2,1)S(1)} all-gather(bf16[1,6,384]{2,1,0:T(8,128)(2,1)S(1)} %bitcast.146), channel_id=1, replica_groups=mesh['fsdp'=32,'feat'=4] {'fsdp'}, dimensions={0}, use_global_device_ids=true | all-gather | bytes 152064 | tf_op jit(solution)/shard_map/all_gather | solution.py:126
  339.6 5.1 %multiply_reduce_fusion = f32[12,128,2]{2,0,1:T(8,128)} fusion(bf16[128,12,1,2,192]{4,3,1,0,2:T(2,128)(2,1)S(1)} %bitcast.137, f32[12,128,2]{2,0,1:T(8,128)S(1)} %broadcast_multiply_fusion), kind=kLoop, calls=%fused_computation.188 | loop fusion | flops 2356224 | bytes 1204224 | tf_op jit(solution)/shard_map/reduce_sum | solution.py:17
  347.3 3.4 reshape.240
  350.8 3.4 reshape.239
  362.0 5.6 %fusion.235 = f32[3072,192]{0,1:T(8,128)} fusion(bf16[384,192]{1,0:T(8,128)(2,1)S(1)} %reshape.249, bf16[192,384]{1,0:T(8,128)(2,1)S(1)} %reshape.247, f32[3072,192]{1,0:T(8,128)} %reshape.240, f32[192]{0:T(256)S(1)} %bitcast.149, f32[3072]{0:T(1024)S(1)} %rsqrt.30, f32[3072]{0:T(1024)S(1)} %div.133), kind=kOutput, calls=%fused_computation.226 | convolution fusion | flops 918945792 | bytes 5038848 | tf_op jit(solution)/shard_map/dot_general | solution.py:109
  (159 shorter events, 177.1 us)
Async XLA Ops:
  0.0 29.8 %copy-start.18 = (f32[3,192]{1,0:T(4,128)S(1)}, f32[3,192]{1,0:T(4,128)}, u32[]{:S(2)}) copy-start(f32[3,192]{1,0:T(4,128)} %param.13) | copy-start | bytes 6916
  0.0 30.4 %copy-start.2 = (bf16[12,256,192]{1,2,0:T(8,128)(2,1)S(1)}, bf16[12,256,192]{1,2,0:T(8,128)(2,1)}, u32[]{:S(2)}) copy-start(bf16[12,256,192]{1,2,0:T(8,128)(2,1)} %param.9) | copy-start | bytes 3538948
  40.0 3.8 %copy-start.7 = (bf16[1,192,192]{2,0,1:T(2,128)(2,1)S(1)}, bf16[1,192,192]{2,0,1:T(2,128)(2,1)}, u32[]{:S(2)}) copy-start(bf16[1,192,192]{2,0,1:T(2,128)(2,1)} %get-tuple-element.118) | copy-start | bytes 221188
  64.7 2.9 copy-start.15
  67.6 2.4 copy-start.14
  67.6 2.9 copy-start.24
  72.6 2.0 copy-start.22
  82.6 9.4 %copy-start.6 = (bf16[1,192,192]{2,0,1:T(2,128)(2,1)S(1)}, bf16[1,192,192]{2,0,1:T(2,128)(2,1)}, u32[]{:S(2)}) copy-start(bf16[1,192,192]{2,0,1:T(2,128)(2,1)} %get-tuple-element.113) | copy-start | bytes 221188
  84.9 32.1 %all-to-all-start = ((bf16[12,128,2,192]{3,2,0,1:T(2,128)(2,1)}), bf16[12,128,2,192]{3,2,0,1:T(2,128)(2,1)S(1)}, u32[]{:S(2)}, u32[]{:S(2)}) async-start(bf16[12,128,2,192]{3,2,0,1:T(2,128)(2,1)} %copy.182), calls=%async_computation | async-start | bytes 3145728 | tf_op jit(solution)/shard_map/all_to_all | solution.py:140
  117.0 6.0 %copy-start = (bf16[12,128,2,192]{3,2,0,1:T(2,128)(2,1)}, bf16[12,128,2,192]{3,2,0,1:T(2,128)(2,1)S(1)}, u32[]{:S(2)}) copy-start(bf16[12,128,2,192]{3,2,0,1:T(2,128)(2,1)S(1)} %all-to-all-done) | copy-start | bytes 3538948
  123.1 5.4 %copy-start.10 = (bf16[1,192,192]{2,0,1:T(2,128)(2,1)S(1)}, bf16[1,192,192]{2,0,1:T(2,128)(2,1)}, u32[]{:S(2)}) copy-start(bf16[1,192,192]{2,0,1:T(2,128)(2,1)} %get-tuple-element.120) | copy-start | bytes 221188
  131.9 7.1 %copy-start.9 = (bf16[1,192,192]{2,0,1:T(2,128)(2,1)S(1)}, bf16[1,192,192]{2,0,1:T(2,128)(2,1)}, u32[]{:S(2)}) copy-start(bf16[1,192,192]{2,0,1:T(2,128)(2,1)} %get-tuple-element.119) | copy-start | bytes 221188
  142.3 7.0 %copy-start.8 = (bf16[1,192,192]{2,0,1:T(2,128)(2,1)S(1)}, bf16[1,192,192]{2,0,1:T(2,128)(2,1)}, u32[]{:S(2)}) copy-start(bf16[1,192,192]{2,0,1:T(2,128)(2,1)} %get-tuple-element.114) | copy-start | bytes 221188
  153.5 3.1 copy-start.5
  188.6 3.1 copy-start.5
  223.6 3.1 copy-start.5
  258.4 2.5 copy-start.1
  261.9 3.4 copy-start.11
  267.8 6.8 %copy-start.16 = (bf16[12,192]{1,0:T(8,128)(2,1)S(1)}, bf16[12,192]{1,0:T(8,128)(2,1)}, u32[]{:S(2)}) copy-start(bf16[12,192]{1,0:T(8,128)(2,1)} %param.12) | copy-start | bytes 13828
  267.8 46.0 %copy-start.17 = (bf16[6,384]{1,0:T(8,128)(2,1)S(1)}, bf16[6,384]{1,0:T(8,128)(2,1)}, u32[]{:S(2)}) copy-start(bf16[6,384]{1,0:T(8,128)(2,1)} %param.11) | copy-start | bytes 13828
  270.7 66.0 %all-to-all-start.1 = ((bf16[1536,1,2,192]{3,2,1,0:T(2,128)(2,1)}), bf16[1536,1,2,192]{3,2,1,0:T(2,128)(2,1)S(1)}, u32[]{:S(2)}, u32[]{:S(2)}) async-start(bf16[1536,1,2,192]{3,2,1,0:T(2,128)(2,1)} %copy.195), calls=%async_computation.1 | async-start | bytes 3145728 | tf_op jit(solution)/shard_map/all_to_all | solution.py:148
  354.2 5.6 %copy-start.3 = (f32[12,256,192]{2,1,0:T(8,128)S(1)}, f32[12,256,192]{2,1,0:T(8,128)}, u32[]{:S(2)}) copy-start(f32[12,256,192]{2,1,0:T(8,128)} %reshape.239) | copy-start | bytes 7077892
  358.3 3.7 copy-start.19
  362.0 5.6 %copy-start.4 = (f32[12,256,192]{1,2,0:T(8,128)S(1)}, f32[12,256,192]{1,2,0:T(8,128)}, u32[]{:S(2)}) copy-start(f32[12,256,192]{1,2,0:T(8,128)} %copy.203) | copy-start | bytes 7077892
  (5 other events, 7.7 us)
where the time goes:
time: 378 us; the launch traced here: 371 us
  matrix products  143 us (38%)
  blocking collectives  89.6 us (24%)
  local copies, waits for them, and re-layouts  74.2 us (20%)
  other arithmetic  26.4 us (7%)
  waiting for transfers between devices  24.1 us (6%)
  starting transfers between devices  11 us (3%)
    sub x24, matrix products, softmax_rows(): exponent = jnp.exp(masked - row_maximum)  62.1 us
    dot_general x18, matrix products, one_block(): jnp.einsum('tdj,jtn->dtn', attention_probabilities, value_rows[..., train...  59.2 us
    all_gather x1, blocking collectives, local(): lax.all_gather(hidden_down_weight, 'fsdp', axis=0, tiled=True)  39.1 us
    all_gather x1, blocking collectives, local(): lax.all_gather(attn_weights, 'fsdp', axis=1, tiled=True)  27.7 us
    all_to_all x1, waiting for transfers between devices, local(): lax.all_to_all(split_cells, ('fsdp', 'feat'), split_axis=1, concat_axis=0...  24.1 us
    all_gather x1, blocking collectives, local(): lax.all_gather(hidden_up_weight, 'fsdp', axis=0, tiled=True)  22.8 us
    unnamed x55, local copies, waits for them, and re-layouts  18.9 us
    reshape x5, local copies, waits for them, and re-layouts, project(): product.astype(jnp.bfloat16).reshape(normed.shape[:-1] + (weight.shape[1],))  10.6 us
  transfers between devices with their start and end apart: 2, of which 1 were waited for; matrix products, arithmetic and copies ran while one was open for 0% of the time, Pallas kernels for 0%

commit v1 on v0

v1 whole, which is shorter than its diff:
```python
import functools

import jax
import jax.numpy as jnp
from jax import lax
from jax.experimental import pallas as pl
from jax.experimental.pallas import tpu as pltpu
from jax.sharding import PartitionSpec as P

MESH = pl.DeviceIdType.MESH
HEADS = 6
EPS = 1e-05
NEGATIVE = -1e30
EXT = 48
MSG = 40
F32 = jnp.float32
BF16 = jnp.bfloat16
VMEM = pl.BlockSpec(memory_space=pltpu.VMEM)
SMEM = pl.BlockSpec(memory_space=pltpu.SMEM)


def norm_t(cells_t, gain):
    mean = jnp.mean(cells_t, axis=0, keepdims=True)
    centered = cells_t - mean
    var = jnp.mean(centered * centered, axis=0, keepdims=True)
    return (centered * lax.rsqrt(var + EPS) * gain).astype(BF16)


def dot(a, b):
    return jnp.dot(a, b, preferred_element_type=F32)


def first_row(count, top):
    rows = lax.broadcasted_iota(jnp.int32, (16, count), 0)
    return jnp.where(rows == 0, top, 0.0).astype(F32)


def wait_all(ref, count, sem):
    blocks = ref.at[pl.ds(0, count)]
    pltpu.make_async_copy(blocks, blocks, sem).wait()


def gather_kernel(n, shard_ref, full_ref, send, recv, own_sem):
    me, feat = lax.axis_index("fsdp"), lax.axis_index("feat")
    barrier = pltpu.get_barrier_semaphore()

    @pl.loop(1, n)
    def _(k):
        pl.semaphore_signal(
            barrier, inc=1, device_id=(lax.rem(me + k, n), feat), device_id_type=MESH
        )

    own = pltpu.make_async_copy(shard_ref, full_ref.at[me], own_sem)
    own.start()
    pl.semaphore_wait(barrier, n - 1)

    def copy(k):
        return pltpu.make_async_remote_copy(
            src_ref=shard_ref,
            dst_ref=full_ref.at[me],
            send_sem=send,
            recv_sem=recv,
            device_id=(lax.rem(me + k, n), feat),
            device_id_type=MESH,
        )

    @pl.loop(1, n)
    def _(k):
        copy(k).start()

    own.wait()
    wait_all(full_ref, n - 1, send)
    wait_all(full_ref, n - 1, recv)


def gather(shard, n):
    return pl.pallas_call(
        functools.partial(gather_kernel, n),
        out_shape=jax.ShapeDtypeStruct((n,) + shard.shape, shard.dtype),
        in_specs=[VMEM],
        out_specs=VMEM,
        scratch_shapes=[pltpu.SemaphoreType.DMA] * 3,
        compiler_params=pltpu.CompilerParams(
            collective_id=0, has_side_effects=True, vmem_limit_bytes=40 * 2**20
        ),
        name="gather_weights",
    )(shard)


def stack_weights(full_ref, first, last, scratch, out_ref):
    n, rows, _ = full_ref.shape
    for i in range(n):
        scratch[pl.ds(i * rows, rows), :] = full_ref[i, :, first:last].astype(F32)
    for c in range(0, last - first, 128):
        out_ref[c : c + 128, :] = scratch[:, c : c + 128].T.astype(BF16)


def feature_kernel(
    count_ref, x_ref, full_ref, gains_ref, out_ref, w_f32, w_ref, cells
):
    rows, feats, width = x_ref.shape
    head = width // HEADS
    scale = head**-0.5 * 1.4426950408889634
    stack_weights(full_ref, 0, 4 * width, w_f32, w_ref)
    live = lax.broadcasted_iota(jnp.int32, (1, feats), 1) < count_ref[0]
    mask = first_row(feats, jnp.where(live, 0.0, NEGATIVE))
    ones = first_row(feats, 1.0)
    ones_b = ones.astype(BF16)
    gain = gains_ref[:, 0:1]

    def row(r, carry):
        x_t = x_ref[r].astype(F32).T
        normed = norm_t(x_t, gain)
        qkv = dot(w_ref[0 : 3 * width, :], normed)
        heads = []
        for h in range(HEADS):
            q = (qkv[h * head : (h + 1) * head] * scale).astype(BF16)
            q = jnp.concatenate([q, ones_b], axis=0)
            k = jnp.concatenate([qkv[width + h * head : width + (h + 1) * head], mask], axis=0)
            k = k.T.astype(BF16)
            v = qkv[2 * width + h * head : 2 * width + (h + 1) * head].astype(BF16)
            v = jnp.concatenate([v, ones_b], axis=0)
            s = dot(k, q)
            p = jnp.exp2(s - jnp.max(s, axis=0, keepdims=True)).astype(BF16)
            o = dot(v, p)
            heads.append((o[:head] / o[head : head + 1]).astype(BF16))
        y = dot(w_ref[3 * width : 4 * width, :], jnp.concatenate(heads, axis=0)) + x_t
        half = feats // 2
        y = jnp.concatenate([y[:, :half], y[:, half:]], axis=0)
        for t in range(3):
            cells[pl.ds(t * rows + r, half, stride=MSG), :] = y[t * 128 : (t + 1) * 128].T
        return carry

    lax.fori_loop(0, rows, row, 0)

    def pack(d, carry):
        at = pl.multiple_of(d * MSG, 8)
        out_ref[d] = cells[pl.ds(at, MSG), :].astype(BF16)
        return carry

    lax.fori_loop(0, feats // 2, pack, 0, unroll=4)


def feature_part(count, x, full, gains_t, devices):
    rows, feats, width = x.shape
    return pl.pallas_call(
        feature_kernel,
        out_shape=jax.ShapeDtypeStruct((devices, MSG, 128), BF16),
        in_specs=[SMEM, VMEM, VMEM, VMEM],
        out_specs=VMEM,
        scratch_shapes=[
            pltpu.VMEM((width, 4 * width), F32),
            pltpu.VMEM((4 * width, width), BF16),
            pltpu.VMEM((devices * MSG, 128), F32),
        ],
        compiler_params=pltpu.CompilerParams(vmem_limit_bytes=50 * 2**20),
        name="feature_attention",
    )(count, x, full, gains_t)


def position(fsdp, feat, k, groups, devices):
    d = lax.rem(fsdp * groups + feat + k, devices)
    return d // groups, lax.rem(d, groups)


def exchange(groups, devices, src_ref, dst_ref, send, recv, own_sem):
    fsdp, feat = lax.axis_index("fsdp"), lax.axis_index("feat")
    me = fsdp * groups + feat
    barrier = pltpu.get_barrier_semaphore()

    @pl.loop(1, devices)
    def _(k):
        pl.semaphore_signal(
            barrier, inc=1, device_id=position(fsdp, feat, k, groups, devices), device_id_type=MESH
        )

    own = pltpu.make_async_copy(src_ref.at[me], dst_ref.at[me], own_sem)
    own.start()
    pl.semaphore_wait(barrier, devices - 1)

    def copy(k):
        to = position(fsdp, feat, k, groups, devices)
        return pltpu.make_async_remote_copy(
            src_ref=src_ref.at[to[0] * groups + to[1]],
            dst_ref=dst_ref.at[me],
            send_sem=send,
            recv_sem=recv,
            device_id=to,
            device_id_type=MESH,
        )

    @pl.loop(1, devices)
    def _(k):
        copy(k).start()

    own.wait()
    wait_all(dst_ref, devices - 1, send)
    wait_all(dst_ref, devices - 1, recv)


def all_to_all(messages, groups):
    return pl.pallas_call(
        functools.partial(exchange, groups, messages.shape[0]),
        out_shape=jax.ShapeDtypeStruct(messages.shape, messages.dtype),
        in_specs=[VMEM],
        out_specs=VMEM,
        scratch_shapes=[pltpu.SemaphoreType.DMA] * 3,
        compiler_params=pltpu.CompilerParams(
            collective_id=1, has_side_effects=True, vmem_limit_bytes=40 * 2**20
        ),
        name="to_columns",
    )(messages)


def sample_kernel(
    block_q, block_k, count_ref, in_ref, full_ref, gains_ref, out_ref,
    w_f32, w_ref, cells, x_t, q_all, k_all, v_all, acc, top, out_t,
):
    devices = in_ref.shape[0]
    total = cells.shape[1]
    rows = total // devices
    width = gains_ref.shape[0]
    head = width // HEADS
    scale = head**-0.5 * 1.4426950408889634
    stack_weights(full_ref, 4 * width, 12 * width, w_f32, w_ref)

    def unpack(i, carry):
        for j in range(2):
            block = in_ref[2 * i + j].astype(F32)
            at = pl.multiple_of(i * 2 * rows, 8)
            for t in range(3):
                cells[t, pl.ds(at + j * rows, rows), :] = block[t * rows : (t + 1) * rows]
        return carry

    lax.fori_loop(0, devices // 2, unpack, 0, unroll=2)
    for t in range(3):
        for c in range(0, total, 128):
            x_t[t * 128 : (t + 1) * 128, c : c + 128] = cells[t, c : c + 128, :].T
    gain2, gain3 = gains_ref[:, 1:2], gains_ref[:, 2:3]
    ones = first_row(block_q, 1.0).astype(BF16)
    live_blocks = lax.div(count_ref[0] + (block_k - 1), block_k)

    for f in range(2):
        base = f * width

        def project(b, carry):
            at = pl.multiple_of(b * block_q, 128)
            lanes = pl.ds(at, block_q)
            normed = norm_t(x_t[base : base + width, lanes], gain2)
            qkv = dot(w_ref[0 : 3 * width, :], normed)
            live = lax.broadcasted_iota(jnp.int32, (1, block_q), 1) + at < count_ref[0]
            mask = first_row(block_q, jnp.where(live, 0.0, NEGATIVE))
            for h in range(HEADS):
                q = (qkv[h * head : (h + 1) * head] * scale).astype(BF16)
                q_all[h, :, lanes] = jnp.concatenate([q, ones], axis=0)
                k = jnp.concatenate([qkv[width + h * head : width + (h + 1) * head], mask], axis=0)
                k_all[h, lanes, :] = k.T.astype(BF16)
                v = qkv[2 * width + h * head : 2 * width + (h + 1) * head].astype(BF16)
                v_all[h, :, lanes] = jnp.concatenate([v, ones], axis=0)
            return carry

        lax.fori_loop(0, total // block_q, project, 0)

        def queries(b, carry):
            lanes = pl.ds(pl.multiple_of(b * block_q, 128), block_q)
            acc[...] = jnp.zeros_like(acc)
            top[...] = jnp.full_like(top, NEGATIVE)

            def keys(j, inner):
                span = pl.ds(pl.multiple_of(j * block_k, 128), block_k)
                for h in range(HEADS):
                    s = dot(k_all[h, span, :], q_all[h, :, lanes])
                    before = top[h : h + 1]
                    now = jnp.maximum(before, jnp.max(s, axis=0, keepdims=True))
                    p = jnp.exp2(s - now).astype(BF16)
                    top[h : h + 1] = now
                    acc[h] = acc[h] * jnp.exp2(before - now) + dot(v_all[h, :, span], p)
                return inner

            lax.fori_loop(0, live_blocks, keys, 0)
            heads = [(acc[h, :head] / acc[h, head : head + 1]).astype(BF16) for h in range(HEADS)]
            y = dot(w_ref[3 * width : 4 * width, :], jnp.concatenate(heads, axis=0))
            sampled = (y + x_t[base : base + width, lanes]).astype(BF16).astype(F32)
            normed = norm_t(sampled, gain3)
            hidden = jax.nn.gelu(dot(w_ref[4 * width : 6 * width, :], normed)).astype(BF16)
            y = dot(w_ref[6 * width : 7 * width, :], hidden[:width])
            y += dot(w_ref[7 * width : 8 * width, :], hidden[width:])
            out_t[base : base + width, lanes] = sampled + y
            return carry

        lax.fori_loop(0, total // block_q, queries, 0)

    for t in range(3):
        for c in range(0, total, 128):
            cells[t, c : c + 128, :] = out_t[t * 128 : (t + 1) * 128, c : c + 128].T

    def pack(i, carry):
        for j in range(2):
            at = pl.multiple_of(i * 2 * rows, 8)
            for t in range(3):
                out_ref[2 * i + j, t * rows : (t + 1) * rows, :] = cells[
                    t, pl.ds(at + j * rows, rows), :
                ].astype(BF16)
        return carry

    lax.fori_loop(0, devices // 2, pack, 0, unroll=2)


def sample_part(count, columns, full, gains_t, total):
    width = gains_t.shape[0]
    block_q, block_k = 512, 128
    return pl.pallas_call(
        functools.partial(sample_kernel, block_q, block_k),
        out_shape=jax.ShapeDtypeStruct(columns.shape, BF16),
        in_specs=[SMEM, VMEM, VMEM, VMEM],
        out_specs=VMEM,
        scratch_shapes=[
            pltpu.VMEM((width, 8 * width), F32),
            pltpu.VMEM((8 * width, width), BF16),
            pltpu.VMEM((3, total, 128), F32),
            pltpu.VMEM((2 * width, total), F32),
            pltpu.VMEM((HEADS, EXT, total), BF16),
            pltpu.VMEM((HEADS, total, EXT), BF16),
            pltpu.VMEM((HEADS, EXT, total), BF16),
            pltpu.VMEM((HEADS, EXT, block_q), F32),
            pltpu.VMEM((8, block_q), F32),
            pltpu.VMEM((2 * width, total), F32),
        ],
        compiler_params=pltpu.CompilerParams(vmem_limit_bytes=56 * 2**20),
        name="sample_attention",
    )(count, columns, full, gains_t)


def back_kernel(groups, devices, src_ref, out_ref, landed, cells, send, recv, own_sem):
    rows, feats, width = out_ref.shape
    half = feats // 2
    exchange(groups, devices, src_ref, landed, send, recv, own_sem)

    def unpack(d, carry):
        cells[pl.ds(pl.multiple_of(d * MSG, 8), MSG), :] = landed[d].astype(F32)
        return carry

    lax.fori_loop(0, devices, unpack, 0, unroll=4)

    def row(r, carry):
        a, b, c = (cells[pl.ds(t * rows + r, half, stride=MSG), :] for t in range(3))
        out_ref[r, :half, :128] = a.astype(BF16)
        out_ref[r, :half, 128:] = b[:, :64].astype(BF16)
        out_ref[r, half:, :] = jnp.concatenate([b[:, 64:], c], axis=1).astype(BF16)
        return carry

    lax.fori_loop(0, rows, row, 0)


def back_to_rows(messages, groups, shape):
    devices = messages.shape[0]
    return pl.pallas_call(
        functools.partial(back_kernel, groups, devices),
        out_shape=jax.ShapeDtypeStruct(shape, BF16),
        in_specs=[VMEM],
        out_specs=VMEM,
        scratch_shapes=[
            pltpu.VMEM(messages.shape, BF16),
            pltpu.VMEM((devices * MSG, 128), F32),
            *[pltpu.SemaphoreType.DMA] * 3,
        ],
        compiler_params=pltpu.CompilerParams(
            collective_id=2, has_side_effects=True, vmem_limit_bytes=40 * 2**20
        ),
        name="back_to_rows",
    )(messages)


def local(table_cells, attn, up, down, norm_gains, train_count, feature_count):
    rows, feats, width = table_cells.shape
    n, groups = lax.axis_size("fsdp"), lax.axis_size("feat")
    devices = n * groups
    part = width // n
    shard = jnp.concatenate(
        [
            jnp.swapaxes(attn, 0, 1).reshape(part, 8 * width),
            jnp.swapaxes(up.reshape(part, width, 2), 1, 2).reshape(part, 2 * width),
            down.reshape(part, 2 * width),
        ],
        axis=1,
    )
    full = gather(shard, n)
    gains_t = norm_gains.T
    messages = feature_part(feature_count, table_cells, full, gains_t, devices)
    columns = all_to_all(messages, groups)
    done = sample_part(train_count, columns, full, gains_t, rows * devices)
    return back_to_rows(done, groups, table_cells.shape)


def solution(mesh):
    in_specs = (
        P(("fsdp", "feat"), None, None),
        P(None, "fsdp", None),
        P("fsdp", None),
        P("fsdp", None),
        P(),
        P(),
        P(),
    )
    out_specs = P(("fsdp", "feat"), None, None)
    return jax.shard_map(local, mesh=mesh, in_specs=in_specs, out_specs=out_specs, check_vma=False)
```

time: 378 us -> 199 us (0.53); the launches traced: 371 us -> 198 us
  Pallas kernels: 0 us -> 188 us
  matrix products: 143 us -> 0 us
  blocking collectives: 89.6 us -> 0 us
  local copies, waits for them, and re-layouts: 74.2 us -> 8.35 us
  other arithmetic: 26.4 us -> 0.01 us
  waiting for transfers between devices: 24.1 us -> 0 us
  starting transfers between devices: 11 us -> 0 us
    pallas_call x0 -> x5, Pallas kernels: none -> 188 us  [the longest x1 77.8 us: sample_part(): pl.pallas_call(functools.partial(sample_kernel, block_q, block_k), out_sh...]
    all_gather x3 -> x0, blocking collectives: 89.6 us -> none  [the longest x1 39.1 us: local(): lax.all_gather(hidden_down_weight, 'fsdp', axis=0, tiled=True)]
    dot_general x33 -> x0, matrix products: 81.4 us -> none  [the longest x18 59.2 us: one_block(): jnp.einsum('tdj,jtn->dtn', attention_probabilities, value_rows[..., train...]
    sub x24 -> x0, matrix products: 62.1 us -> none  [softmax_rows(): exponent = jnp.exp(masked - row_maximum)]
    all_to_all x2 -> x0, waiting for transfers between devices: 24.1 us -> none  [the longest x1 24.1 us: local(): lax.all_to_all(split_cells, ('fsdp', 'feat'), split_axis=1, concat_axis=0...]
    convert_element_type x10 -> x0, local copies, waits for them, and re-layouts: 20.9 us -> none  [the longest x4 10.5 us: feed_forward(): value_rows.astype(jnp.float32)]
    reshape x9 -> x3, local copies, waits for them, and re-layouts: 16.6 us -> 1.71 us  [the longest x1 0.84 us: local(): jnp.swapaxes(attn, 0, 1).reshape(part, 8 * width)]
    unnamed x55 -> x15, local copies, waits for them, and re-layouts: 18.9 us -> 5.02 us
  transfers between devices with their start and end apart: 2 -> 0, of which waited for: 1 -> 0; matrix products, arithmetic and copies ran while one was open for 0% -> 0% of each run, Pallas kernels for 0% -> 0%
where the time goes in v1:
time: 199 us; the launch traced here: 198 us
  Pallas kernels  188 us (94%)
  local copies, waits for them, and re-layouts  8.35 us (4%)
    pallas_call x1, Pallas kernels, sample_part(): pl.pallas_call(functools.partial(sample_kernel, block_q, block_k), out_sh...  77.8 us
    pallas_call x1, Pallas kernels, feature_part(): pl.pallas_call(feature_kernel, out_shape=jax.ShapeDtypeStruct((devices, M...  30.2 us
    pallas_call x1, Pallas kernels, all_to_all(): pl.pallas_call(functools.partial(exchange, groups, messages.shape[0]), ou...  28 us
    pallas_call x1, Pallas kernels, back_to_rows(): pl.pallas_call(functools.partial(back_kernel, groups, devices), out_shape...  27.8 us
    pallas_call x1, Pallas kernels, gather(): pl.pallas_call(functools.partial(gather_kernel, n), out_shape=jax.ShapeDt...  24.5 us
    unnamed x15, local copies, waits for them, and re-layouts  5.02 us

profile of v1, /device:TPU:1, one launch (start us, length us, event | category | flops | bytes accessed | tf_op | source)
XLA Modules:
  0.0 198.1 jit_solution(14984003498430089054)
XLA Ops:
  0.0 0.0 copy-start.5
  0.0 0.0 copy-start.4
  0.0 1.0 copy.12
  1.0 0.1 copy.13
  1.1 0.1 reshape.14
  1.2 0.8 reshape.12
  2.0 0.8 reshape.15
  2.8 24.5 %gather_weights.1.full_ref = bf16[32,6,2304]{2,1,0:T(8,128)(2,1)S(1)} custom-call(bf16[6,2304]{1,0:T(8,128)(2,1)S(1)} %pad_maximum_fusion.shard_ref), custom_call_target="tpu_custom_call" | custom-call | tf_op jit(solution)/shard_map/gather_weights/pallas_call | solution.py:77
  27.3 0.0 copy-done.5
  27.3 0.0 copy-start
  27.3 0.1 copy.14
  27.4 0.0 copy-start.3
  27.5 0.0 copy-done.4
  27.5 1.6 copy.15.x_ref
  29.7 0.0 copy-done
  29.7 0.0 copy-done.3
  29.7 30.2 %feature_attention.1.src_ref = bf16[128,40,128]{2,1,0:T(8,128)(2,1)S(1)} custom-call(s32[1]{0:T(128)S(6)} %copy.18.count_ref, bf16[12,256,192]{2,1,0:T(8,128)(2,1)} %copy.15.x_ref, bf16[32,6,2304]{2,1,0:T(8,128)(2,1)S(1)} %gather_weights.1.full_ref, f32[192,3]{1,0:T(8,128)S(1)} %bitcast.5), custom_call_target="tpu_custom_call" | custom-call | tf_op jit(solution)/shard_map/feature_attention/pallas_call | solution.py:146
  59.9 28.0 %to_columns.1.in_ref = bf16[128,40,128]{2,1,0:T(8,128)(2,1)S(1)} custom-call(bf16[128,40,128]{2,1,0:T(8,128)(2,1)S(1)} %feature_attention.1.src_ref), custom_call_target="tpu_custom_call" | custom-call | tf_op jit(solution)/shard_map/to_columns/pallas_call | solution.py:202
  87.9 0.0 copy-start.1
  88.0 1.1 copy-done.1
  89.7 77.8 %sample_attention.1.src_ref = bf16[128,40,128]{2,1,0:T(8,128)(2,1)} custom-call(s32[1]{0:T(128)S(6)} %copy.17.count_ref, bf16[128,40,128]{2,1,0:T(8,128)(2,1)} %copy-done.1, bf16[32,6,2304]{2,1,0:T(8,128)(2,1)} %copy-done, f32[192,3]{1,0:T(8,128)} %bitcast.6), custom_call_target="tpu_custom_call" | custom-call | tf_op jit(solution)/shard_map/sample_attention/pallas_call | solution.py:312
  167.5 1.3 copy-done.2
  168.8 27.8 %back_to_rows.1 = bf16[12,256,192]{2,1,0:T(8,128)(2,1)S(1)} custom-call(bf16[128,40,128]{2,1,0:T(8,128)(2,1)S(1)} %copy-done.2), custom_call_target="tpu_custom_call" | custom-call | tf_op jit(solution)/shard_map/back_to_rows/pallas_call | solution.py:357
  196.6 1.5 copy.16
  (2 shorter events, 0.0 us)
Async XLA Ops:
  0.0 27.3 %copy-start.5 = (f32[3,192]{1,0:T(4,128)S(1)}, f32[3,192]{1,0:T(4,128)}, u32[]{:S(2)}) copy-start(f32[3,192]{1,0:T(4,128)} %param.11) | copy-start | bytes 6916
  0.0 27.5 %copy-start.4 = (bf16[12,256,192]{1,2,0:T(8,128)(2,1)S(1)}, bf16[12,256,192]{1,2,0:T(8,128)(2,1)}, u32[]{:S(2)}) copy-start(bf16[12,256,192]{1,2,0:T(8,128)(2,1)} %param.7) | copy-start | bytes 3538948
  27.3 2.4 %copy-start = (bf16[32,6,2304]{2,1,0:T(8,128)(2,1)}, bf16[32,6,2304]{2,1,0:T(8,128)(2,1)S(1)}, u32[]{:S(2)}) copy-start(bf16[32,6,2304]{2,1,0:T(8,128)(2,1)S(1)} %gather_weights.1.full_ref) | copy-start | bytes 2654212
  27.4 2.2 %copy-start.3 = (f32[3,192]{0,1:T(8,128)}, f32[3,192]{0,1:T(8,128)S(1)}, u32[]{:S(2)}) copy-start(f32[3,192]{0,1:T(8,128)S(1)} %copy.14) | copy-start | bytes 6916
  87.9 1.1 copy-start.1
  167.5 1.3 copy-start.2

commit v2 on v1

--- a/solution.py
+++ b/solution.py
@@ -13,6 +13,7 @@
 NEGATIVE = -1e30
 EXT = 48
 MSG = 40
+EARLY = 8
 F32 = jnp.float32
 BF16 = jnp.bfloat16
 VMEM = pl.BlockSpec(memory_space=pltpu.VMEM)
@@ -87,80 +88,177 @@
     )(shard)
 
 
-def stack_weights(full_ref, first, last, scratch, out_ref):
+def stack_weights(full_ref, first, last, scratch, out_ref, between=None):
     n, rows, _ = full_ref.shape
     for i in range(n):
         scratch[pl.ds(i * rows, rows), :] = full_ref[i, :, first:last].astype(F32)
+        if between is not None:
+            between(i)
     for c in range(0, last - first, 128):
         out_ref[c : c + 128, :] = scratch[:, c : c + 128].T.astype(BF16)
 
 
+def position(fsdp, feat, k, groups, devices):
+    d = lax.rem(fsdp * groups + feat + k, devices)
+    return d // groups, lax.rem(d, groups)
+
+
 def feature_kernel(
-    count_ref, x_ref, full_ref, gains_ref, out_ref, w_f32, w_ref, cells
+    groups, devices, count_ref, x_ref, full_ref, shard_ref, gains_ref,
+    early_ref, late_ref, rest_ref, w_f32, w_ref, cells_a, cells_b, out_a, out_b, send, recv, own,
 ):
     rows, feats, width = x_ref.shape
     head = width // HEADS
+    half = feats // 2
+    n = devices // groups
     scale = head**-0.5 * 1.4426950408889634
-    stack_weights(full_ref, 0, 4 * width, w_f32, w_ref)
+    fsdp, feat = lax.axis_index("fsdp"), lax.axis_index("feat")
+    me = fsdp * groups + feat
+    barrier = pltpu.get_barrier_semaphore()
+    each = devices // n
+
+    def greet(i):
+        for k in range(max(1, i * each), (i + 1) * each):
+            pl.semaphore_signal(
+                barrier, inc=1, device_id=position(fsdp, feat, k, groups, devices),
+                device_id_type=MESH,
+            )
+
+    stack_weights(full_ref, 0, 4 * width, w_f32, w_ref, greet)
     live = lax.broadcasted_iota(jnp.int32, (1, feats), 1) < count_ref[0]
     mask = first_row(feats, jnp.where(live, 0.0, NEGATIVE))
-    ones = first_row(feats, 1.0)
-    ones_b = ones.astype(BF16)
+    ones_b = first_row(feats, 1.0).astype(BF16)
     gain = gains_ref[:, 0:1]
 
-    def row(r, carry):
-        x_t = x_ref[r].astype(F32).T
-        normed = norm_t(x_t, gain)
-        qkv = dot(w_ref[0 : 3 * width, :], normed)
+    def two_rows(i, cells, stride, height, skip):
+        x_t = jnp.concatenate([x_ref[2 * i + j].astype(F32).T for j in range(2)], axis=1)
+        qkv = dot(w_ref[0 : 3 * width, :], norm_t(x_t, gain))
+
+        def part(unit, kind):
+            j, h = unit // HEADS, unit % HEADS
+            at = kind * width + h * head
+            return qkv[at : at + head, j * feats : (j + 1) * feats]
+
+        def score(unit):
+            q = jnp.concatenate([(part(unit, 0) * scale).astype(BF16), ones_b], axis=0)
+            k = jnp.concatenate([part(unit, 1), mask], axis=0).T.astype(BF16)
+            return dot(k, q)
+
         heads = []
-        for h in range(HEADS):
-            q = (qkv[h * head : (h + 1) * head] * scale).astype(BF16)
-            q = jnp.concatenate([q, ones_b], axis=0)
-            k = jnp.concatenate([qkv[width + h * head : width + (h + 1) * head], mask], axis=0)
-            k = k.T.astype(BF16)
-            v = qkv[2 * width + h * head : 2 * width + (h + 1) * head].astype(BF16)
-            v = jnp.concatenate([v, ones_b], axis=0)
-            s = dot(k, q)
+        s = score(0)
+        for unit in range(2 * HEADS):
+            following = score(unit + 1) if unit + 1 < 2 * HEADS else None
             p = jnp.exp2(s - jnp.max(s, axis=0, keepdims=True)).astype(BF16)
-            o = dot(v, p)
+            o = dot(jnp.concatenate([part(unit, 2).astype(BF16), ones_b], axis=0), p)
             heads.append((o[:head] / o[head : head + 1]).astype(BF16))
-        y = dot(w_ref[3 * width : 4 * width, :], jnp.concatenate(heads, axis=0)) + x_t
-        half = feats // 2
-        y = jnp.concatenate([y[:, :half], y[:, half:]], axis=0)
-        for t in range(3):
-            cells[pl.ds(t * rows + r, half, stride=MSG), :] = y[t * 128 : (t + 1) * 128].T
-        return carry
-
-    lax.fori_loop(0, rows, row, 0)
-
-    def pack(d, carry):
-        at = pl.multiple_of(d * MSG, 8)
-        out_ref[d] = cells[pl.ds(at, MSG), :].astype(BF16)
-        return carry
-
-    lax.fori_loop(0, feats // 2, pack, 0, unroll=4)
-
-
-def feature_part(count, x, full, gains_t, devices):
+            s = following
+        heads = jnp.concatenate(
+            [jnp.concatenate(heads[:HEADS], axis=0), jnp.concatenate(heads[HEADS:], axis=0)], axis=1
+        )
+        y = dot(w_ref[3 * width : 4 * width, :], heads) + x_t
+        for j in range(2):
+            at = j * feats
+            m = jnp.concatenate([y[:, at : at + half], y[:, at + half : at + feats]], axis=0)
+            for t in range(3):
+                cells[pl.ds(t * height + 2 * i + j - skip, half, stride=stride), :] = m[
+                    t * 128 : (t + 1) * 128
+                ].T
+
+    def send_rest(k):
+        pltpu.make_async_remote_copy(
+            src_ref=shard_ref, dst_ref=rest_ref.at[fsdp],
+            send_sem=send.at[0], recv_sem=recv.at[0],
+            device_id=(lax.rem(fsdp + k, n), feat), device_id_type=MESH,
+        ).start()
+
+    def send_cells(k, src, dst, which):
+        to = position(fsdp, feat, k, groups, devices)
+        pltpu.make_async_remote_copy(
+            src_ref=src.at[to[0] * groups + to[1]], dst_ref=dst.at[me],
+            send_sem=send.at[which], recv_sem=recv.at[which],
+            device_id=to, device_id_type=MESH,
+        ).start()
+
+    def pack(cells, out, d):
+        stride = cells.shape[0] // devices
+        at = pl.multiple_of(d * stride, 8)
+        out[d] = cells[pl.ds(at, out.shape[1]), :].astype(BF16)
+
+    early = lambda i: two_rows(i, cells_a, 3 * EARLY, EARLY, 0)
+    late = lambda i: two_rows(i, cells_b, 16, rows - EARLY, EARLY)
+
+    early(0)
+    own_rest = pltpu.make_async_copy(shard_ref, rest_ref.at[fsdp], own.at[0])
+    own_rest.start()
+    pl.semaphore_wait(barrier, devices - 1)
+
+    @pl.loop(1, n)
+    def _(k):
+        send_rest(k)
+
+    @pl.loop(1, EARLY // 2)
+    def _(i):
+        early(i)
+
+    pack(cells_a, out_a, me)
+    own_a = pltpu.make_async_copy(out_a.at[me], early_ref.at[me], own.at[1])
+    own_a.start()
+
+    @pl.loop(1, devices)
+    def _(k):
+        pack(cells_a, out_a, lax.rem(me + k, devices))
+        send_cells(k, out_a, early_ref, 1)
+
+    @pl.loop(EARLY // 2, rows // 2)
+    def _(i):
+        late(i)
+
+    pack(cells_b, out_b, me)
+    own_b = pltpu.make_async_copy(out_b.at[me], late_ref.at[me], own.at[2])
+    own_b.start()
+
+    @pl.loop(1, devices)
+    def _(k):
+        pack(cells_b, out_b, lax.rem(me + k, devices))
+        send_cells(k, out_b, late_ref, 2)
+
+    own_rest.wait()
+    own_a.wait()
+    own_b.wait()
+    for which, ref in enumerate((rest_ref, early_ref, late_ref)):
+        wait_all(ref, ref.shape[0] - 1, send.at[which])
+        wait_all(ref, ref.shape[0] - 1, recv.at[which])
+
+
+def feature_part(count, x, full, shard, gains_t, groups, devices):
     rows, feats, width = x.shape
+    n = devices // groups
+    early, late = (devices, 3 * EARLY, 128), (devices, 3 * (rows - EARLY), 128)
     return pl.pallas_call(
-        feature_kernel,
-        out_shape=jax.ShapeDtypeStruct((devices, MSG, 128), BF16),
-        in_specs=[SMEM, VMEM, VMEM, VMEM],
-        out_specs=VMEM,
+        functools.partial(feature_kernel, groups, devices),
+        out_shape=[
+            jax.ShapeDtypeStruct(early, BF16),
+            jax.ShapeDtypeStruct(late, BF16),
+            jax.ShapeDtypeStruct((n,) + shard.shape, BF16),
+        ],
+        in_specs=[SMEM, VMEM, VMEM, VMEM, VMEM],
+        out_specs=[VMEM] * 3,
         scratch_shapes=[
             pltpu.VMEM((width, 4 * width), F32),
             pltpu.VMEM((4 * width, width), BF16),
-            pltpu.VMEM((devices * MSG, 128), F32),
+            pltpu.VMEM((devices * 3 * EARLY, 128), F32),
+            pltpu.VMEM((devices * 16, 128), F32),
+            pltpu.VMEM(early, BF16),
+            pltpu.VMEM(late, BF16),
+            pltpu.SemaphoreType.DMA((3,)),
+            pltpu.SemaphoreType.DMA((3,)),
+            pltpu.SemaphoreType.DMA((3,)),
         ],
-        compiler_params=pltpu.CompilerParams(vmem_limit_bytes=50 * 2**20),
+        compiler_params=pltpu.CompilerParams(
+            collective_id=1, has_side_effects=True, vmem_limit_bytes=50 * 2**20
+        ),
         name="feature_attention",
-    )(count, x, full, gains_t)
-
-
-def position(fsdp, feat, k, groups, devices):
-    d = lax.rem(fsdp * groups + feat + k, devices)
-    return d // groups, lax.rem(d, groups)
+    )(count, x, full, shard, gains_t)
 
 
 def exchange(groups, devices, src_ref, dst_ref, send, recv, own_sem):
@@ -198,38 +296,26 @@
     wait_all(dst_ref, devices - 1, recv)
 
 
-def all_to_all(messages, groups):
-    return pl.pallas_call(
-        functools.partial(exchange, groups, messages.shape[0]),
-        out_shape=jax.ShapeDtypeStruct(messages.shape, messages.dtype),
-        in_specs=[VMEM],
-        out_specs=VMEM,
-        scratch_shapes=[pltpu.SemaphoreType.DMA] * 3,
-        compiler_params=pltpu.CompilerParams(
-            collective_id=1, has_side_effects=True, vmem_limit_bytes=40 * 2**20
-        ),
-        name="to_columns",
-    )(messages)
-
-
 def sample_kernel(
-    block_q, block_k, count_ref, in_ref, full_ref, gains_ref, out_ref,
+    block_q, block_k, count_ref, early_ref, late_ref, full_ref, gains_ref, out_ref,
     w_f32, w_ref, cells, x_t, q_all, k_all, v_all, acc, top, out_t,
 ):
-    devices = in_ref.shape[0]
+    devices = early_ref.shape[0]
     total = cells.shape[1]
     rows = total // devices
     width = gains_ref.shape[0]
     head = width // HEADS
     scale = head**-0.5 * 1.4426950408889634
-    stack_weights(full_ref, 4 * width, 12 * width, w_f32, w_ref)
+    stack_weights(full_ref, 0, 8 * width, w_f32, w_ref)
 
     def unpack(i, carry):
         for j in range(2):
-            block = in_ref[2 * i + j].astype(F32)
-            at = pl.multiple_of(i * 2 * rows, 8)
-            for t in range(3):
-                cells[t, pl.ds(at + j * rows, rows), :] = block[t * rows : (t + 1) * rows]
+            at = pl.multiple_of(i * 2 * rows, 8) + j * rows
+            for ref, first, last in ((early_ref, 0, EARLY), (late_ref, EARLY, rows)):
+                block = ref[2 * i + j].astype(F32)
+                count = last - first
+                for t in range(3):
+                    cells[t, pl.ds(at + first, count), :] = block[t * count : (t + 1) * count]
         return carry
 
     lax.fori_loop(0, devices // 2, unpack, 0, unroll=2)
@@ -268,13 +354,18 @@
 
             def keys(j, inner):
                 span = pl.ds(pl.multiple_of(j * block_k, 128), block_k)
+                def score(h):
+                    return dot(k_all[h, span, :], q_all[h, :, lanes])
+
+                s = score(0)
                 for h in range(HEADS):
-                    s = dot(k_all[h, span, :], q_all[h, :, lanes])
+                    following = score(h + 1) if h + 1 < HEADS else None
                     before = top[h : h + 1]
                     now = jnp.maximum(before, jnp.max(s, axis=0, keepdims=True))
                     p = jnp.exp2(s - now).astype(BF16)
                     top[h : h + 1] = now
                     acc[h] = acc[h] * jnp.exp2(before - now) + dot(v_all[h, :, span], p)
+                    s = following
                 return inner
 
             lax.fori_loop(0, live_blocks, keys, 0)
@@ -306,13 +397,14 @@
     lax.fori_loop(0, devices // 2, pack, 0, unroll=2)
 
 
-def sample_part(count, columns, full, gains_t, total):
+def sample_part(count, early, late, full, gains_t, total):
     width = gains_t.shape[0]
-    block_q, block_k = 512, 128
+    devices = early.shape[0]
+    block_q, block_k = 512, 384
     return pl.pallas_call(
         functools.partial(sample_kernel, block_q, block_k),
-        out_shape=jax.ShapeDtypeStruct(columns.shape, BF16),
-        in_specs=[SMEM, VMEM, VMEM, VMEM],
+        out_shape=jax.ShapeDtypeStruct((devices, MSG, 128), BF16),
+        in_specs=[SMEM, VMEM, VMEM, VMEM, VMEM],
         out_specs=VMEM,
         scratch_shapes=[
             pltpu.VMEM((width, 8 * width), F32),
@@ -328,7 +420,7 @@
         ],
         compiler_params=pltpu.CompilerParams(vmem_limit_bytes=56 * 2**20),
         name="sample_attention",
-    )(count, columns, full, gains_t)
+    )(count, early, late, full, gains_t)
 
 
 def back_kernel(groups, devices, src_ref, out_ref, landed, cells, send, recv, own_sem):
@@ -376,19 +468,21 @@
     n, groups = lax.axis_size("fsdp"), lax.axis_size("feat")
     devices = n * groups
     part = width // n
-    shard = jnp.concatenate(
+    attn = jnp.swapaxes(attn, 0, 1).reshape(part, 8 * width)
+    rest = jnp.concatenate(
         [
-            jnp.swapaxes(attn, 0, 1).reshape(part, 8 * width),
+            attn[:, 4 * width :],
             jnp.swapaxes(up.reshape(part, width, 2), 1, 2).reshape(part, 2 * width),
             down.reshape(part, 2 * width),
         ],
         axis=1,
     )
-    full = gather(shard, n)
+    full = gather(attn[:, : 4 * width], n)
     gains_t = norm_gains.T
-    messages = feature_part(feature_count, table_cells, full, gains_t, devices)
-    columns = all_to_all(messages, groups)
-    done = sample_part(train_count, columns, full, gains_t, rows * devices)
+    early, late, rest = feature_part(
+        feature_count, table_cells, full, rest, gains_t, groups, devices
+    )
+    done = sample_part(train_count, early, late, rest, gains_t, rows * devices)
     return back_to_rows(done, groups, table_cells.shape)
 
 

time: 199 us -> 136 us (0.68)
  Pallas kernels: 188 us -> 123 us
  local copies, waits for them, and re-layouts: 8.35 us -> 11.5 us
    pallas_call x1, Pallas kernels: 77.8 us -> 44.5 us  [sample_part(): pl.pallas_call(functools.partial(sample_kernel, block_q, block_k), out_sh...]
    pallas_call x2 -> x1, Pallas kernels: 58.2 us -> 34.7 us  [feature_part(): pl.pallas_call(functools.partial(feature_kernel, groups, devices), out_sh...]
    pallas_call x1, Pallas kernels: 24.5 us -> 14.6 us  [gather(): pl.pallas_call(functools.partial(gather_kernel, n), out_shape=jax.ShapeDt...]
    unnamed x15 -> x13, local copies, waits for them, and re-layouts: 5.02 us -> 8.13 us
where the time goes in v2:
time: 136 us
  Pallas kernels  123 us (90%)
  local copies, waits for them, and re-layouts  11.5 us (8%)
  between operations  1.38 us (1%)
    pallas_call x1, Pallas kernels, sample_part(): pl.pallas_call(functools.partial(sample_kernel, block_q, block_k), out_sh...  44.5 us
    pallas_call x1, Pallas kernels, feature_part(): pl.pallas_call(functools.partial(feature_kernel, groups, devices), out_sh...  34.7 us
    pallas_call x1, Pallas kernels, back_to_rows(): pl.pallas_call(functools.partial(back_kernel, groups, devices), out_shape...  29.1 us
    pallas_call x1, Pallas kernels, gather(): pl.pallas_call(functools.partial(gather_kernel, n), out_shape=jax.ShapeDt...  14.6 us
    unnamed x13, local copies, waits for them, and re-layouts  8.13 us

profile of v2, /device:TPU:1, one launch (start us, length us, event | category | flops | bytes accessed | tf_op | source)
XLA Modules:
  0.0 135.7 jit_solution(2177586497554024576)
XLA Ops:
  0.0 0.8 reshape.12
  0.8 14.6 %gather_weights.1.full_ref = bf16[32,6,768]{2,1,0:T(8,128)(2,1)S(1)} custom-call(bf16[6,768]{1,0:T(8,128)(2,1)S(1)} %get-tuple-element.12.shard_ref), custom_call_target="tpu_custom_call" | custom-call | tf_op jit(solution)/shard_map/gather_weights/pallas_call | solution.py:78
  15.4 0.9 copy.12
  16.3 0.1 copy.13
  16.4 0.1 reshape.14
  16.5 0.8 reshape.15
  17.3 0.8 copy.14
  18.1 0.0 copy-start.1
  18.1 2.6 %copy.15.x_ref = bf16[12,256,192]{2,1,0:T(8,128)(2,1)} copy(bf16[12,256,192]{1,2,0:T(8,128)(2,1)} %param.7) | data formatting | bytes 2359296 | tf_op args[0]
  21.3 0.0 copy-done.1
  21.3 34.7 %feature_attention.1 = (bf16[128,24,128]{2,1,0:T(8,128)(2,1)S(1)}, bf16[128,12,128]{2,1,0:T(8,128)(2,1)S(1)}, bf16[32,6,1536]{2,1,0:T(8,128)(2,1)S(1)}) custom-call(s32[1]{0:T(128)S(6)} %copy.18.count_ref, bf16[12,256,192]{2,1,0:T(8,128)(2,1)} %copy.15.x_ref, bf16[32,6,768]{2,1,0:T(8,128)(2,1)S(1)} %gather_weights.1.full_ref, ...), custom_call_target="tpu_custom_call" | custom-call | tf_op jit(solution)/shard_map/feature_attention/pallas_call | solution.py:237
  56.0 0.0 copy-start.2
  56.1 0.9 copy-done.2
  56.9 0.0 copy-start.3
  56.9 0.9 copy-done.3
  57.8 0.0 copy-start.4
  57.8 0.8 copy-done.4
  59.3 44.5 %sample_attention.1.src_ref = bf16[128,40,128]{2,1,0:T(8,128)(2,1)} custom-call(s32[1]{0:T(128)S(6)} %copy.17.count_ref, bf16[128,24,128]{2,1,0:T(8,128)(2,1)} %copy-done.2, bf16[128,12,128]{2,1,0:T(8,128)(2,1)} %copy-done.4, bf16[32,6,1536]{2,1,0:T(8,128)(2,1)} %copy-done.3, f32[192,3]{1,0:T(8,128)} %bitcast.6), custom_call_target="tpu_custom_call" | custom-call | tf_op jit(solution)/shard_map/sample_attention/pallas_call | solution.py:404
  103.8 0.0 copy-start
  103.8 1.3 copy-done
  105.1 29.1 %back_to_rows.1 = bf16[12,256,192]{2,1,0:T(8,128)(2,1)S(1)} custom-call(bf16[128,40,128]{2,1,0:T(8,128)(2,1)S(1)} %copy-done), custom_call_target="tpu_custom_call" | custom-call | tf_op jit(solution)/shard_map/back_to_rows/pallas_call | solution.py:449
  134.2 1.5 %copy.16 = bf16[12,256,192]{1,2,0:T(8,128)(2,1)} copy(bf16[12,256,192]{2,1,0:T(8,128)(2,1)S(1)} %back_to_rows.1) | data formatting | bytes 2359296 | tf_op jit(solution)/shard_map/back_to_rows/pallas_call | solution.py:449
  (2 shorter events, 0.0 us)
Async XLA Ops:
  18.1 3.2 %copy-start.1 = (f32[3,192]{0,1:T(8,128)}, f32[3,192]{0,1:T(8,128)S(1)}, u32[]{:S(2)}) copy-start(f32[3,192]{0,1:T(8,128)S(1)} %copy.14) | copy-start | bytes 6916
  56.0 0.9 copy-start.2
  56.9 0.9 copy-start.3
  57.8 0.8 copy-start.4
  103.8 1.3 copy-start

commit v3 on v0

v3 whole, which is shorter than its diff:
```python
import functools

import jax
import jax.numpy as jnp
from jax import lax
from jax.experimental import pallas as pl
from jax.experimental.pallas import tpu as pltpu
from jax.sharding import PartitionSpec as P

MESH = pl.DeviceIdType.MESH
HEADS = 6
EPS = 1e-05
NEGATIVE = -1e30
EXT = 48
MSG = 40
EARLY = 8
F32 = jnp.float32
BF16 = jnp.bfloat16
VMEM = pl.BlockSpec(memory_space=pltpu.VMEM)
HBM = pl.BlockSpec(memory_space=pl.ANY)
SMEM = pl.BlockSpec(memory_space=pltpu.SMEM)


def norm_t(cells_t, gain):
    mean = jnp.mean(cells_t, axis=0, keepdims=True)
    centered = cells_t - mean
    var = jnp.mean(centered * centered, axis=0, keepdims=True)
    return (centered * lax.rsqrt(var + EPS) * gain).astype(BF16)


def dot(a, b):
    return jnp.dot(a, b, preferred_element_type=F32)


def first_row(count, top):
    rows = lax.broadcasted_iota(jnp.int32, (16, count), 0)
    return jnp.where(rows == 0, top, 0.0).astype(F32)


def wait_all(ref, count, sem):
    blocks = ref.at[pl.ds(0, count)]
    pltpu.make_async_copy(blocks, blocks, sem).wait()


def position(fsdp, feat, k, groups, devices):
    d = lax.rem(fsdp * groups + feat + k, devices)
    return d // groups, lax.rem(d, groups)


def layer_kernel(
    groups, devices, extent, block,
    x_hbm, attn_ref, up_ref, down_ref, gains_ref, train_ref, feat_ref, out_ref,
    x_ref, rest_f32, x_all, normed_all, first_shard, rest_shard, first_full, rest_full,
    w_f32, d_f32, w_one, w_two, w_down, cells_a, cells_b, out_a, out_b, early_ref, late_ref,
    cells, x_t, q_all, k_all, v_all, out_t, packed, landed, spread,
    w_send, w_recv, own, send, recv, back_send, back_recv,
):
    rows, feats, width = x_ref.shape
    head = width // HEADS
    half = feats // 2
    n = devices // groups
    part = width // n
    total = rows * devices
    scale = head**-0.5 * 1.4426950408889634
    fsdp, feat = lax.axis_index("fsdp"), lax.axis_index("feat")
    me = fsdp * groups + feat

    fetch = pltpu.make_async_copy(x_hbm, x_ref, own.at[0])
    fetch.start()
    barrier = pltpu.get_barrier_semaphore()

    @pl.loop(1, devices)
    def _(k):
        pl.semaphore_signal(
            barrier, inc=1, device_id=position(fsdp, feat, k, groups, devices), device_id_type=MESH
        )

    def beside(*parts):
        return jnp.concatenate([v.astype(F32) for v in parts], axis=1).astype(BF16)

    first_shard[...] = beside(*(attn_ref[i] for i in range(4)))
    rest_shard[...] = beside(
        *(attn_ref[i] for i in range(4, 8)), up_ref[...], down_ref[:part], down_ref[part:]
    )
    own_first = pltpu.make_async_copy(first_shard, first_full.at[fsdp], own.at[1])
    own_first.start()
    own_rest = pltpu.make_async_copy(rest_shard, rest_full.at[fsdp], own.at[2])
    own_rest.start()
    gains_t = jnp.concatenate([gains_ref[...], jnp.zeros((5, width), F32)], axis=0).T
    gain1, gain2, gain3 = (gains_t[:, i : i + 1] for i in range(3))

    def send_shard(k, src, dst, which):
        pltpu.make_async_remote_copy(
            src_ref=src, dst_ref=dst.at[fsdp], send_sem=w_send.at[which], recv_sem=w_recv.at[which],
            device_id=(lax.rem(fsdp + k, n), feat), device_id_type=MESH,
        ).start()

    pl.semaphore_wait(barrier, devices - 1)

    @pl.loop(1, n)
    def _(k):
        send_shard(k, first_shard, first_full, 0)

    fetch.wait()

    @pl.loop(0, rows // 2)
    def _(i):
        cells_t = jnp.concatenate([x_ref[2 * i + j].astype(F32).T for j in range(2)], axis=1)
        x_all[i] = cells_t
        normed_all[i] = norm_t(cells_t, gain1)

    own_first.wait()
    wait_all(first_full, n - 1, w_recv.at[0])

    @pl.loop(1, n)
    def _(k):
        send_shard(k, rest_shard, rest_full, 1)

    for i in range(n):
        w_f32[pl.ds(i * part, part), :] = first_full[i].astype(F32)
    for c in range(0, 4 * width, 128):
        w_one[c : c + 128, :] = w_f32[:, c : c + 128].T.astype(BF16)

    live = lax.broadcasted_iota(jnp.int32, (1, feats), 1) < feat_ref[0]
    mask = first_row(feats, jnp.where(live, 0.0, NEGATIVE))
    ones_b = first_row(feats, 1.0).astype(BF16)

    def two_rows(i, into, stride, height, skip):
        qkv = dot(w_one[0 : 3 * width, :], normed_all[i])

        def piece(unit, kind):
            j, h = unit // HEADS, unit % HEADS
            at = kind * width + h * head
            return qkv[at : at + head, j * feats : (j + 1) * feats]

        def score(unit):
            q = jnp.concatenate([(piece(unit, 0) * scale).astype(BF16), ones_b], axis=0)
            k = jnp.concatenate([piece(unit, 1), mask], axis=0).T.astype(BF16)
            return dot(k, q)

        heads = []
        s = score(0)
        for unit in range(2 * HEADS):
            following = score(unit + 1) if unit + 1 < 2 * HEADS else None
            p = jnp.exp2(s - jnp.max(s, axis=0, keepdims=True)).astype(BF16)
            o = dot(jnp.concatenate([piece(unit, 2).astype(BF16), ones_b], axis=0), p)
            heads.append((o[:head] / o[head : head + 1]).astype(BF16))
            s = following
        heads = jnp.concatenate(
            [jnp.concatenate(heads[:HEADS], axis=0), jnp.concatenate(heads[HEADS:], axis=0)], axis=1
        )
        y = dot(w_one[3 * width : 4 * width, :], heads) + x_all[i]
        for j in range(2):
            at = j * feats
            m = jnp.concatenate([y[:, at : at + half], y[:, at + half : at + feats]], axis=0)
            for t in range(3):
                into[pl.ds(t * height + 2 * i + j - skip, half, stride=stride), :] = m[
                    t * 128 : (t + 1) * 128
                ].T

    def pack(source, out, d):
        stride = source.shape[0] // devices
        at = pl.multiple_of(d * stride, 8)
        out[d] = source[pl.ds(at, out.shape[1]), :].astype(BF16)

    def send_cells(k, src, dst, which):
        to = position(fsdp, feat, k, groups, devices)
        pltpu.make_async_remote_copy(
            src_ref=src.at[to[0] * groups + to[1]], dst_ref=dst.at[me],
            send_sem=send.at[which], recv_sem=recv.at[which],
            device_id=to, device_id_type=MESH,
        ).start()

    @pl.loop(0, EARLY // 2)
    def _(i):
        two_rows(i, cells_a, 3 * EARLY, EARLY, 0)

    pack(cells_a, out_a, me)
    own_a = pltpu.make_async_copy(out_a.at[me], early_ref.at[me], own.at[3])
    own_a.start()

    @pl.loop(1, devices)
    def _(k):
        pack(cells_a, out_a, lax.rem(me + k, devices))
        send_cells(k, out_a, early_ref, 0)

    @pl.loop(EARLY // 2, rows // 2)
    def _(i):
        two_rows(i, cells_b, 16, rows - EARLY, EARLY)

    pack(cells_b, out_b, me)
    own_b = pltpu.make_async_copy(out_b.at[me], late_ref.at[me], own.at[4])
    own_b.start()

    @pl.loop(1, devices)
    def _(k):
        pack(cells_b, out_b, lax.rem(me + k, devices))
        send_cells(k, out_b, late_ref, 1)

    own_rest.wait()
    wait_all(rest_full, n - 1, w_recv.at[1])
    down_at = 6 * width
    for i in range(n):
        shard = rest_full[i].astype(F32)
        rest_f32[pl.ds(i * part, part), :] = shard[:, :down_at]
        for j in range(2):
            at = down_at + j * width
            d_f32[pl.ds((2 * i + j) * part, part), :] = shard[:, at : at + width]
    for c in range(0, down_at, 128):
        w_two[c : c + 128, :] = rest_f32[:, c : c + 128].T.astype(BF16)
    w_down[...] = d_f32[...].T.astype(BF16)

    def unpack(ref, first, last):
        count = last - first

        @pl.loop(0, devices // 2, unroll=2)
        def _(i):
            for j in range(2):
                received = ref[2 * i + j].astype(F32)
                at = pl.multiple_of(i * 2 * rows, 8) + j * rows + first
                for t in range(3):
                    cells[t, pl.ds(at, count), :] = received[t * count : (t + 1) * count]

    own_a.wait()
    wait_all(early_ref, devices - 1, recv.at[0])
    unpack(early_ref, 0, EARLY)
    own_b.wait()
    wait_all(late_ref, devices - 1, recv.at[1])
    unpack(late_ref, EARLY, rows)

    blocks = total // block
    peers = devices // blocks
    plane, place = me // peers, lax.rem(me, peers)
    for t in range(3):
        for c in range(0, total, 128):
            x_t[t * 128 : (t + 1) * 128, c : c + 128] = cells[t, c : c + 128, :].T
    ones = first_row(block, 1.0).astype(BF16)

    def project(step, with_keys):
        f, b = lax.rem(step, 2), step // 2
        at = pl.multiple_of(b * block, 128)
        lanes = pl.ds(at, block)
        base = pl.multiple_of(f * width, 8)
        normed = norm_t(x_t[pl.ds(base, width), lanes], gain2)
        qkv = dot(w_two[0 : (3 if with_keys else 1) * width, :], normed)
        live = lax.broadcasted_iota(jnp.int32, (1, block), 1) + at < train_ref[0]
        mask = first_row(block, jnp.where(live, 0.0, NEGATIVE))
        for h in range(HEADS):
            q = (qkv[h * head : (h + 1) * head] * scale).astype(BF16)
            q_all[f, h, :, lanes] = jnp.concatenate([q, ones], axis=0)
            if with_keys:
                k = jnp.concatenate([qkv[width + h * head : width + (h + 1) * head], mask], axis=0)
                k_all[f, h, lanes, :] = k.T.astype(BF16)
                v = qkv[2 * width + h * head : 2 * width + (h + 1) * head].astype(BF16)
                v_all[f, h, :, lanes] = jnp.concatenate([v, ones], axis=0)

    key_blocks = -(-extent // block)

    @pl.loop(0, 2 * key_blocks)
    def _(step):
        project(step, True)

    @pl.loop(2 * key_blocks, 2 * blocks)
    def _(step):
        project(step, False)

    def attend(b, f):
        lanes = pl.ds(pl.multiple_of(b * block, 128), block)
        base = pl.multiple_of(f * width, 8)

        def score(h):
            return dot(k_all[f, h, :extent, :], q_all[f, h, :, lanes])

        heads = []
        s = score(0)
        for h in range(HEADS):
            following = score(h + 1) if h + 1 < HEADS else None
            p = jnp.exp2(s - jnp.max(s, axis=0, keepdims=True)).astype(BF16)
            o = dot(v_all[f, h, :, :extent], p)
            heads.append((o[:head] / o[head : head + 1]).astype(BF16))
            s = following
        y = dot(w_two[3 * width : 4 * width, :], jnp.concatenate(heads, axis=0))
        sampled = (y + x_t[pl.ds(base, width), lanes]).astype(BF16).astype(F32)
        normed = norm_t(sampled, gain3)
        hidden = jax.nn.gelu(dot(w_two[4 * width : 6 * width, :], normed)).astype(BF16)
        out_t[pl.ds(base, width), :] = sampled + dot(w_down[...], hidden)

    def prepare(b):
        @pl.loop(0, 2)
        def _(f):
            attend(b, f)

        for t in range(3):
            for c in range(0, block, 128):
                cells[t, c : c + 128, :] = out_t[t * 128 : (t + 1) * 128, c : c + 128].T

        @pl.loop(0, peers // 2)
        def _(i):
            for j in range(2):
                at = pl.multiple_of(i * 2 * rows, 8) + j * rows
                for t in range(3):
                    packed[b * peers + 2 * i + j, t * rows : (t + 1) * rows, :] = cells[
                        t, pl.ds(at, rows), :
                    ].astype(BF16)

    def send_back(b, k, which):
        to = b * peers + lax.rem(place + k, peers)
        pltpu.make_async_remote_copy(
            src_ref=packed.at[to], dst_ref=landed.at[me],
            send_sem=back_send.at[which], recv_sem=back_recv.at[which],
            device_id=(to // groups, lax.rem(to, groups)), device_id_type=MESH,
        ).start()

    def place_group(source, count, which):
        wait_all(landed, count, back_recv.at[which])
        base = source * peers

        @pl.loop(0, peers, unroll=4)
        def _(d):
            spread[pl.ds(pl.multiple_of(d * MSG, 8), 3 * rows), :] = landed[base + d].astype(F32)

        low = pl.ds(pl.multiple_of(base, 16), peers)
        high = pl.ds(pl.multiple_of(half + base, 16), peers)

        @pl.loop(0, rows)
        def _(r):
            u, v, w = (spread[pl.ds(t * rows + r, peers, stride=MSG), :] for t in range(3))
            out_ref[r, low, :] = jnp.concatenate([u, v[:, :64]], axis=1).astype(BF16)
            out_ref[r, high, :] = jnp.concatenate([v[:, 64:], w], axis=1).astype(BF16)

    order = [blocks // 2] + [i for i in range(1, blocks) if i != blocks // 2] + [0]
    last = len(order) - 1
    for which, shift in enumerate(order[:-1]):
        b = lax.rem(plane + shift, blocks)
        prepare(b)

        @pl.loop(0, peers)
        def _(k):
            send_back(b, k, which)

    prepare(plane)
    own_back = pltpu.make_async_copy(packed.at[me], landed.at[me], own.at[5])
    own_back.start()

    @pl.loop(1, peers)
    def _(k):
        send_back(plane, k, last)

    for which, shift in enumerate(order[:-1]):
        place_group(lax.rem(plane + blocks - shift, blocks), peers, which)
    own_back.wait()
    place_group(plane, peers - 1, last)

    wait_all(first_full, n - 1, w_send.at[0])
    wait_all(rest_full, n - 1, w_send.at[1])
    wait_all(early_ref, devices - 1, send.at[0])
    wait_all(late_ref, devices - 1, send.at[1])
    for which in range(len(order)):
        wait_all(packed, peers if which < last else peers - 1, back_send.at[which])


def local(table_cells, attn, up, down, norm_gains, train_count, feature_count):
    rows, feats, width = table_cells.shape
    n, groups = lax.axis_size("fsdp"), lax.axis_size("feat")
    devices = n * groups
    part = width // n
    total = rows * devices
    blocks = 4
    block = total // blocks
    extent = total * 3 // 4
    early, late = (devices, 3 * EARLY, 128), (devices, 3 * (rows - EARLY), 128)
    message = (devices, 3 * rows, 128)
    vmem = pltpu.VMEM
    return pl.pallas_call(
        functools.partial(layer_kernel, groups, devices, extent, block),
        out_shape=jax.ShapeDtypeStruct(table_cells.shape, BF16),
        in_specs=[HBM, VMEM, VMEM, VMEM, VMEM, SMEM, SMEM],
        out_specs=VMEM,
        scratch_shapes=[
            vmem(table_cells.shape, BF16),
            vmem((width, 6 * width), F32),
            vmem((rows // 2, width, 2 * feats), F32),
            vmem((rows // 2, width, 2 * feats), BF16),
            vmem((part, 4 * width), BF16),
            vmem((part, 8 * width), BF16),
            vmem((n, part, 4 * width), BF16),
            vmem((n, part, 8 * width), BF16),
            vmem((width, 4 * width), F32),
            vmem((2 * width, width), F32),
            vmem((4 * width, width), BF16),
            vmem((6 * width, width), BF16),
            vmem((width, 2 * width), BF16),
            vmem((devices * 3 * EARLY, 128), F32),
            vmem((devices * 16, 128), F32),
            vmem(early, BF16),
            vmem(late, BF16),
            vmem(early, BF16),
            vmem(late, BF16),
            vmem((3, total, 128), F32),
            vmem((2 * width, total), F32),
            vmem((2, HEADS, EXT, total), BF16),
            vmem((2, HEADS, total, EXT), BF16),
            vmem((2, HEADS, EXT, total), BF16),
            vmem((2 * width, block), F32),
            vmem(message, BF16),
            vmem(message, BF16),
            vmem((devices // blocks * MSG, 128), F32),
            pltpu.SemaphoreType.DMA((2,)),
            pltpu.SemaphoreType.DMA((2,)),
            pltpu.SemaphoreType.DMA((6,)),
            pltpu.SemaphoreType.DMA((2,)),
            pltpu.SemaphoreType.DMA((2,)),
            pltpu.SemaphoreType.DMA((blocks,)),
            pltpu.SemaphoreType.DMA((blocks,)),
        ],
        compiler_params=pltpu.CompilerParams(
            collective_id=0, has_side_effects=True, vmem_limit_bytes=56 * 2**20
        ),
        name="layer",
    )(table_cells, attn, up, down, norm_gains, train_count, feature_count)


def solution(mesh):
    in_specs = (
        P(("fsdp", "feat"), None, None),
        P(None, "fsdp", None),
        P("fsdp", None),
        P("fsdp", None),
        P(),
        P(),
        P(),
    )
    out_specs = P(("fsdp", "feat"), None, None)
    return jax.shard_map(local, mesh=mesh, in_specs=in_specs, out_specs=out_specs, check_vma=False)
```

time: 378 us -> 107 us (0.28); the launches traced: 371 us -> 106 us
  matrix products: 143 us -> 0 us
  Pallas kernels: 0 us -> 98.7 us
  blocking collectives: 89.6 us -> 0 us
  local copies, waits for them, and re-layouts: 74.2 us -> 6.4 us
  other arithmetic: 26.4 us -> 0 us
  waiting for transfers between devices: 24.1 us -> 0 us
  starting transfers between devices: 11 us -> 0 us
    pallas_call x0 -> x1, Pallas kernels: none -> 98.7 us  [local(): pl.pallas_call(functools.partial(layer_kernel, groups, devices, extent, b...]
    all_gather x3 -> x0, blocking collectives: 89.6 us -> none  [the longest x1 39.1 us: local(): lax.all_gather(hidden_down_weight, 'fsdp', axis=0, tiled=True)]
    dot_general x33 -> x0, matrix products: 81.4 us -> none  [the longest x18 59.2 us: one_block(): jnp.einsum('tdj,jtn->dtn', attention_probabilities, value_rows[..., train...]
    sub x24 -> x0, matrix products: 62.1 us -> none  [softmax_rows(): exponent = jnp.exp(masked - row_maximum)]
    all_to_all x2 -> x0, waiting for transfers between devices: 24.1 us -> none  [the longest x1 24.1 us: local(): lax.all_to_all(split_cells, ('fsdp', 'feat'), split_axis=1, concat_axis=0...]
    convert_element_type x10 -> x0, local copies, waits for them, and re-layouts: 20.9 us -> none  [the longest x4 10.5 us: feed_forward(): value_rows.astype(jnp.float32)]
    reshape x9 -> x0, local copies, waits for them, and re-layouts: 16.6 us -> none  [the longest x5 10.6 us: project(): product.astype(jnp.bfloat16).reshape(normed.shape[:-1] + (weight.shape[1],))]
    unnamed x55 -> x2, local copies, waits for them, and re-layouts: 18.9 us -> 3.89 us
  transfers between devices with their start and end apart: 2 -> 0, of which waited for: 1 -> 0; matrix products, arithmetic and copies ran while one was open for 0% -> 0% of each run, Pallas kernels for 0% -> 0%
where the time goes in v3:
time: 107 us; the launch traced here: 106 us
  Pallas kernels  98.7 us (92%)
  local copies, waits for them, and re-layouts  6.4 us (6%)
  between operations  1.31 us (1%)
    pallas_call x1, Pallas kernels, local(): pl.pallas_call(functools.partial(layer_kernel, groups, devices, extent, b...  98.7 us
    unnamed x2, local copies, waits for them, and re-layouts  3.89 us
    pallas_call x1, local copies, waits for them, and re-layouts, local(): pl.pallas_call(functools.partial(layer_kernel, groups, devices, extent, b...  2.51 us

profile of v3, /device:TPU:1, one launch (start us, length us, event | category | flops | bytes accessed | tf_op | source)
XLA Modules:
  0.0 106.4 jit_solution(8386721480432211606)
XLA Ops:
  1.3 1.4 %copy.9.attn_ref = bf16[8,6,192]{2,1,0:T(8,128)(2,1)} copy(bf16[8,6,192]{2,0,1:T(8,128)(2,1)} %param.8) | data formatting | bytes 36864 | tf_op args[1]
  2.7 2.5 %copy.8.x_hbm = bf16[12,256,192]{2,1,0:T(8,128)(2,1)} copy(bf16[12,256,192]{1,2,0:T(8,128)(2,1)} %param.7) | data formatting | bytes 2359296 | tf_op args[0]
  5.2 98.7 %layer.1 = bf16[12,256,192]{2,1,0:T(8,128)(2,1)} custom-call(bf16[12,256,192]{2,1,0:T(8,128)(2,1)} %copy.8.x_hbm, bf16[8,6,192]{2,1,0:T(8,128)(2,1)} %copy.9.attn_ref, bf16[6,384]{1,0:T(8,128)(2,1)} %up_ref.1, bf16[12,192]{1,0:T(8,128)(2,1)} %down_ref.1, f32[3,192]{1,0:T(4,128)} %gains_ref.1, s32[1]{0:T(128)S(6)} %copy.11.train_ref, s32[1]{0:T(128)S(6)} %copy.12.feat_ref), custom_call_target="tpu_custom_call" | custom-call | tf_op jit(solution)/shard_map/layer/pallas_call | solution.py:374
  103.9 2.5 %copy.10 = bf16[12,256,192]{1,2,0:T(8,128)(2,1)} copy(bf16[12,256,192]{2,1,0:T(8,128)(2,1)} %layer.1) | data formatting | bytes 2359296 | tf_op jit(solution)/shard_map/layer/pallas_call | solution.py:374

commit v4 on v3

--- a/solution.py
+++ b/solution.py
@@ -42,6 +42,18 @@
     pltpu.make_async_copy(blocks, blocks, sem).wait()
 
 
+def loop(first, last, body, unroll=8):
+    whole = (last - first) // unroll
+
+    @pl.loop(0, whole)
+    def _(i):
+        for j in range(unroll):
+            body(first + i * unroll + j)
+
+    for k in range(first + whole * unroll, last):
+        body(k)
+
+
 def position(fsdp, feat, k, groups, devices):
     d = lax.rem(fsdp * groups + feat + k, devices)
     return d // groups, lax.rem(d, groups)
@@ -55,7 +67,7 @@
     cells, x_t, q_all, k_all, v_all, out_t, packed, landed, spread,
     w_send, w_recv, own, send, recv, back_send, back_recv,
 ):
-    rows, feats, width = x_ref.shape
+    rows, width, feats = x_ref.shape
     head = width // HEADS
     half = feats // 2
     n = devices // groups
@@ -64,60 +76,70 @@
     scale = head**-0.5 * 1.4426950408889634
     fsdp, feat = lax.axis_index("fsdp"), lax.axis_index("feat")
     me = fsdp * groups + feat
+    chip, core = fsdp // 2, lax.rem(fsdp, 2)
+    chips = n // 2
 
     fetch = pltpu.make_async_copy(x_hbm, x_ref, own.at[0])
     fetch.start()
     barrier = pltpu.get_barrier_semaphore()
 
-    @pl.loop(1, devices)
-    def _(k):
+    def greet(k):
         pl.semaphore_signal(
             barrier, inc=1, device_id=position(fsdp, feat, k, groups, devices), device_id_type=MESH
         )
 
+    loop(1, devices, greet)
+
     def beside(*parts):
         return jnp.concatenate([v.astype(F32) for v in parts], axis=1).astype(BF16)
 
-    first_shard[...] = beside(*(attn_ref[i] for i in range(4)))
+    first_shard[...] = beside(*(attn_ref[:, i] for i in range(4)))
     rest_shard[...] = beside(
-        *(attn_ref[i] for i in range(4, 8)), up_ref[...], down_ref[:part], down_ref[part:]
+        *(attn_ref[:, i] for i in range(4, 8)), up_ref[...], down_ref[:part], down_ref[part:]
     )
-    own_first = pltpu.make_async_copy(first_shard, first_full.at[fsdp], own.at[1])
+    own_first = pltpu.make_async_copy(first_shard, first_full.at[core, chip], own.at[1])
     own_first.start()
-    own_rest = pltpu.make_async_copy(rest_shard, rest_full.at[fsdp], own.at[2])
+    own_rest = pltpu.make_async_copy(rest_shard, rest_full.at[core, chip], own.at[2])
     own_rest.start()
     gains_t = jnp.concatenate([gains_ref[...], jnp.zeros((5, width), F32)], axis=0).T
     gain1, gain2, gain3 = (gains_t[:, i : i + 1] for i in range(3))
 
     def send_shard(k, src, dst, which):
         pltpu.make_async_remote_copy(
-            src_ref=src, dst_ref=dst.at[fsdp], send_sem=w_send.at[which], recv_sem=w_recv.at[which],
-            device_id=(lax.rem(fsdp + k, n), feat), device_id_type=MESH,
+            src_ref=src, dst_ref=dst.at[core, chip],
+            send_sem=w_send.at[which], recv_sem=w_recv.at[which],
+            device_id=(lax.rem(chip + k, chips) * 2 + core, feat), device_id_type=MESH,
         ).start()
 
+    def to_neighbour(full, which):
+        return pltpu.make_async_remote_copy(
+            src_ref=full.at[core], dst_ref=full.at[core],
+            send_sem=w_send.at[which], recv_sem=w_recv.at[which],
+            device_id=(chip * 2 + 1 - core, feat), device_id_type=MESH,
+        )
+
     pl.semaphore_wait(barrier, devices - 1)
 
-    @pl.loop(1, n)
-    def _(k):
-        send_shard(k, first_shard, first_full, 0)
+    loop(1, chips, lambda k: send_shard(k, first_shard, first_full, 0))
 
     fetch.wait()
 
     @pl.loop(0, rows // 2)
     def _(i):
-        cells_t = jnp.concatenate([x_ref[2 * i + j].astype(F32).T for j in range(2)], axis=1)
+        cells_t = jnp.concatenate([x_ref[2 * i + j].astype(F32) for j in range(2)], axis=1)
         x_all[i] = cells_t
         normed_all[i] = norm_t(cells_t, gain1)
 
     own_first.wait()
-    wait_all(first_full, n - 1, w_recv.at[0])
-
-    @pl.loop(1, n)
-    def _(k):
-        send_shard(k, rest_shard, rest_full, 1)
+    wait_all(first_full.at[0], chips - 1, w_recv.at[0])
+    first_pair = to_neighbour(first_full, 1)
+    first_pair.start()
+    first_pair.wait()
 
     for i in range(n):
-        w_f32[pl.ds(i * part, part), :] = first_full[i].astype(F32)
+        w_f32[pl.ds(i * part, part), :] = first_full[i % 2, i // 2].astype(F32)
+        if 0 < i < chips:
+            send_shard(i, rest_shard, rest_full, 2)
     for c in range(0, 4 * width, 128):
         w_one[c : c + 128, :] = w_f32[:, c : c + 128].T.astype(BF16)
 
@@ -175,37 +197,47 @@
     def _(i):
         two_rows(i, cells_a, 3 * EARLY, EARLY, 0)
 
+    own_rest.wait()
+    wait_all(rest_full.at[0], chips - 1, w_recv.at[2])
+    rest_pair = to_neighbour(rest_full, 3)
+    rest_pair.start()
     pack(cells_a, out_a, me)
     own_a = pltpu.make_async_copy(out_a.at[me], early_ref.at[me], own.at[3])
     own_a.start()
 
-    @pl.loop(1, devices)
-    def _(k):
+    def send_early(k):
         pack(cells_a, out_a, lax.rem(me + k, devices))
         send_cells(k, out_a, early_ref, 0)
 
-    @pl.loop(EARLY // 2, rows // 2)
+    late_steps = (rows - EARLY) // 2
+    beside_step = (devices - 1) // late_steps
+    for k in range(1 + late_steps * beside_step, devices):
+        send_early(k)
+
+    @pl.loop(0, late_steps)
     def _(i):
-        two_rows(i, cells_b, 16, rows - EARLY, EARLY)
+        for k in range(beside_step):
+            send_early(1 + i * beside_step + k)
+        two_rows(EARLY // 2 + i, cells_b, 16, rows - EARLY, EARLY)
 
     pack(cells_b, out_b, me)
     own_b = pltpu.make_async_copy(out_b.at[me], late_ref.at[me], own.at[4])
     own_b.start()
 
-    @pl.loop(1, devices)
-    def _(k):
+    def send_late(k):
         pack(cells_b, out_b, lax.rem(me + k, devices))
         send_cells(k, out_b, late_ref, 1)
 
-    own_rest.wait()
-    wait_all(rest_full, n - 1, w_recv.at[1])
+    rest_pair.wait()
     down_at = 6 * width
     for i in range(n):
-        shard = rest_full[i].astype(F32)
+        shard = rest_full[i % 2, i // 2].astype(F32)
         rest_f32[pl.ds(i * part, part), :] = shard[:, :down_at]
         for j in range(2):
             at = down_at + j * width
             d_f32[pl.ds((2 * i + j) * part, part), :] = shard[:, at : at + width]
+        for k in range(max(1, i * groups), (i + 1) * groups):
+            send_late(k)
     for c in range(0, down_at, 128):
         w_two[c : c + 128, :] = rest_f32[:, c : c + 128].T.astype(BF16)
     w_down[...] = d_f32[...].T.astype(BF16)
@@ -213,7 +245,7 @@
     def unpack(ref, first, last):
         count = last - first
 
-        @pl.loop(0, devices // 2, unroll=2)
+        @pl.loop(0, devices // 2, unroll=8)
         def _(i):
             for j in range(2):
                 received = ref[2 * i + j].astype(F32)
@@ -264,37 +296,38 @@
     def _(step):
         project(step, False)
 
-    def attend(b, f):
+    def attend(b):
         lanes = pl.ds(pl.multiple_of(b * block, 128), block)
-        base = pl.multiple_of(f * width, 8)
-
-        def score(h):
+
+        def score(unit):
+            f, h = unit // HEADS, unit % HEADS
             return dot(k_all[f, h, :extent, :], q_all[f, h, :, lanes])
 
         heads = []
         s = score(0)
-        for h in range(HEADS):
-            following = score(h + 1) if h + 1 < HEADS else None
+        for unit in range(2 * HEADS):
+            f, h = unit // HEADS, unit % HEADS
+            following = score(unit + 1) if unit + 1 < 2 * HEADS else None
             p = jnp.exp2(s - jnp.max(s, axis=0, keepdims=True)).astype(BF16)
             o = dot(v_all[f, h, :, :extent], p)
             heads.append((o[:head] / o[head : head + 1]).astype(BF16))
             s = following
-        y = dot(w_two[3 * width : 4 * width, :], jnp.concatenate(heads, axis=0))
-        sampled = (y + x_t[pl.ds(base, width), lanes]).astype(BF16).astype(F32)
-        normed = norm_t(sampled, gain3)
-        hidden = jax.nn.gelu(dot(w_two[4 * width : 6 * width, :], normed)).astype(BF16)
-        out_t[pl.ds(base, width), :] = sampled + dot(w_down[...], hidden)
-
-    def prepare(b):
-        @pl.loop(0, 2)
-        def _(f):
-            attend(b, f)
-
+            if h + 1 < HEADS:
+                continue
+            base = f * width
+            y = dot(w_two[3 * width : 4 * width, :], jnp.concatenate(heads, axis=0))
+            heads = []
+            sampled = (y + x_t[base : base + width, lanes]).astype(BF16).astype(F32)
+            normed = norm_t(sampled, gain3)
+            hidden = jax.nn.gelu(dot(w_two[4 * width : 6 * width, :], normed)).astype(BF16)
+            out_t[base : base + width, :] = sampled + dot(w_down[...], hidden)
+
+    def pack_back(b):
         for t in range(3):
             for c in range(0, block, 128):
                 cells[t, c : c + 128, :] = out_t[t * 128 : (t + 1) * 128, c : c + 128].T
 
-        @pl.loop(0, peers // 2)
+        @pl.loop(0, peers // 2, unroll=8)
         def _(i):
             for j in range(2):
                 at = pl.multiple_of(i * 2 * rows, 8) + j * rows
@@ -311,56 +344,60 @@
             device_id=(to // groups, lax.rem(to, groups)), device_id_type=MESH,
         ).start()
 
-    def place_group(source, count, which):
+    def spread_group(source, count, which):
         wait_all(landed, count, back_recv.at[which])
-        base = source * peers
-
-        @pl.loop(0, peers, unroll=4)
-        def _(d):
-            spread[pl.ds(pl.multiple_of(d * MSG, 8), 3 * rows), :] = landed[base + d].astype(F32)
-
-        low = pl.ds(pl.multiple_of(base, 16), peers)
-        high = pl.ds(pl.multiple_of(half + base, 16), peers)
-
-        @pl.loop(0, rows)
-        def _(r):
-            u, v, w = (spread[pl.ds(t * rows + r, peers, stride=MSG), :] for t in range(3))
-            out_ref[r, low, :] = jnp.concatenate([u, v[:, :64]], axis=1).astype(BF16)
-            out_ref[r, high, :] = jnp.concatenate([v[:, 64:], w], axis=1).astype(BF16)
-
-    order = [blocks // 2] + [i for i in range(1, blocks) if i != blocks // 2] + [0]
-    last = len(order) - 1
-    for which, shift in enumerate(order[:-1]):
-        b = lax.rem(plane + shift, blocks)
-        prepare(b)
-
-        @pl.loop(0, peers)
-        def _(k):
-            send_back(b, k, which)
-
-    prepare(plane)
+
+        @pl.loop(0, peers, unroll=8)
+        def _(i):
+            d = source * peers + i
+            spread[pl.ds(pl.multiple_of(d * MSG, 8), 3 * rows), :] = landed[d].astype(F32)
+
+    last = blocks - 1
+
+    def target(which):
+        return lax.rem(plane + last - which, blocks)
+
+    attend(target(0))
+
+    pack_back(target(0))
+
+    @pl.loop(1, blocks)
+    def _(which):
+        for k in range(peers):
+            send_back(target(which - 1), k, which - 1)
+        attend(target(which))
+
+        pack_back(target(which))
+
     own_back = pltpu.make_async_copy(packed.at[me], landed.at[me], own.at[5])
     own_back.start()
-
-    @pl.loop(1, peers)
-    def _(k):
-        send_back(plane, k, last)
-
-    for which, shift in enumerate(order[:-1]):
-        place_group(lax.rem(plane + blocks - shift, blocks), peers, which)
+    loop(1, peers, lambda k: send_back(plane, k, last))
+
+    for which in range(last):
+        spread_group(lax.rem(plane + 1 + which, blocks), peers, which)
     own_back.wait()
-    place_group(plane, peers - 1, last)
-
-    wait_all(first_full, n - 1, w_send.at[0])
-    wait_all(rest_full, n - 1, w_send.at[1])
+    spread_group(plane, peers - 1, last)
+
+    @pl.loop(0, rows)
+    def _(r):
+        y = jnp.concatenate(
+            [spread[pl.ds(t * rows + r, half, stride=MSG), :].T for t in range(3)], axis=0
+        ).astype(BF16)
+        out_ref[r, :, :half] = y[:width]
+        out_ref[r, :, half:] = y[width:]
+
+
+    wait_all(first_full.at[0], chips - 1, w_send.at[0])
+    wait_all(rest_full.at[0], chips - 1, w_send.at[2])
     wait_all(early_ref, devices - 1, send.at[0])
     wait_all(late_ref, devices - 1, send.at[1])
-    for which in range(len(order)):
+    for which in range(blocks):
         wait_all(packed, peers if which < last else peers - 1, back_send.at[which])
 
 
 def local(table_cells, attn, up, down, norm_gains, train_count, feature_count):
-    rows, feats, width = table_cells.shape
+    table_t, attn = jnp.swapaxes(table_cells, 1, 2), jnp.swapaxes(attn, 0, 1)
+    rows, width, feats = table_t.shape
     n, groups = lax.axis_size("fsdp"), lax.axis_size("feat")
     devices = n * groups
     part = width // n
@@ -371,20 +408,20 @@
     early, late = (devices, 3 * EARLY, 128), (devices, 3 * (rows - EARLY), 128)
     message = (devices, 3 * rows, 128)
     vmem = pltpu.VMEM
-    return pl.pallas_call(
+    layer_t = pl.pallas_call(
         functools.partial(layer_kernel, groups, devices, extent, block),
-        out_shape=jax.ShapeDtypeStruct(table_cells.shape, BF16),
+        out_shape=jax.ShapeDtypeStruct(table_t.shape, BF16),
         in_specs=[HBM, VMEM, VMEM, VMEM, VMEM, SMEM, SMEM],
         out_specs=VMEM,
         scratch_shapes=[
-            vmem(table_cells.shape, BF16),
+            vmem(table_t.shape, BF16),
             vmem((width, 6 * width), F32),
             vmem((rows // 2, width, 2 * feats), F32),
             vmem((rows // 2, width, 2 * feats), BF16),
             vmem((part, 4 * width), BF16),
             vmem((part, 8 * width), BF16),
-            vmem((n, part, 4 * width), BF16),
-            vmem((n, part, 8 * width), BF16),
+            vmem((2, n // 2, part, 4 * width), BF16),
+            vmem((2, n // 2, part, 8 * width), BF16),
             vmem((width, 4 * width), F32),
             vmem((2 * width, width), F32),
             vmem((4 * width, width), BF16),
@@ -404,9 +441,9 @@
             vmem((2 * width, block), F32),
             vmem(message, BF16),
             vmem(message, BF16),
-            vmem((devices // blocks * MSG, 128), F32),
-            pltpu.SemaphoreType.DMA((2,)),
-            pltpu.SemaphoreType.DMA((2,)),
+            vmem((devices * MSG, 128), F32),
+            pltpu.SemaphoreType.DMA((4,)),
+            pltpu.SemaphoreType.DMA((4,)),
             pltpu.SemaphoreType.DMA((6,)),
             pltpu.SemaphoreType.DMA((2,)),
             pltpu.SemaphoreType.DMA((2,)),
@@ -417,7 +454,8 @@
             collective_id=0, has_side_effects=True, vmem_limit_bytes=56 * 2**20
         ),
         name="layer",
-    )(table_cells, attn, up, down, norm_gains, train_count, feature_count)
+    )(table_t, attn, up, down, norm_gains, train_count, feature_count)
+    return jnp.swapaxes(layer_t, 1, 2)
 
 
 def solution(mesh):

time: 107 us -> 97.2 us (0.908)
  Pallas kernels: 98.7 us -> 93.3 us
  local copies, waits for them, and re-layouts: 6.4 us -> 2.36 us
    pallas_call x1, Pallas kernels: 98.7 us -> 93.3 us  [local(): pl.pallas_call(functools.partial(layer_kernel, groups, devices, extent, b...]
    pallas_call x1 -> x0, local copies, waits for them, and re-layouts: 2.51 us -> none  [local(): pl.pallas_call(functools.partial(layer_kernel, groups, devices, extent, b...]
    unnamed x2 -> x1, local copies, waits for them, and re-layouts: 3.89 us -> 2.36 us
where the time goes in v4:
time: 97.2 us; the launch traced here: 97 us
  Pallas kernels  93.3 us (96%)
  local copies, waits for them, and re-layouts  2.36 us (2%)
  between operations  1.31 us (1%)
    pallas_call x1, Pallas kernels, local(): pl.pallas_call(functools.partial(layer_kernel, groups, devices, extent, b...  93.3 us
    unnamed x1, local copies, waits for them, and re-layouts  2.36 us

profile of v4, /device:TPU:1, one launch (start us, length us, event | category | flops | bytes accessed | tf_op | source)
XLA Modules:
  0.0 97.0 jit_solution(10240217075352191697)
XLA Ops:
  1.3 93.3 %layer.1 = bf16[12,192,256]{2,1,0:T(8,128)(2,1)} custom-call(bf16[12,192,256]{2,1,0:T(8,128)(2,1)} %bitcast.4, bf16[6,8,192]{2,1,0:T(8,128)(2,1)} %bitcast.5, bf16[6,384]{1,0:T(8,128)(2,1)} %up_ref.1, bf16[12,192]{1,0:T(8,128)(2,1)} %down_ref.1, f32[3,192]{1,0:T(4,128)} %gains_ref.1, s32[1]{0:T(128)S(6)} %copy.9.train_ref, s32[1]{0:T(128)S(6)} %copy.10.feat_ref), custom_call_target="tpu_custom_call" | custom-call | tf_op jit(solution)/shard_map/layer/pallas_call | solution.py:411
  94.6 2.4 %copy.11 = bf16[12,256,192]{1,2,0:T(8,128)(2,1)} copy(bf16[12,256,192]{1,2,0:T(8,128)(2,1)} %bitcast.3) | data formatting | bytes 2359296
